TPU v7x, 128 devices: a whole 4x4x4 slice. The times are simulated.
128 devices in a mesh: stack: 8 (over y, core), cls: 16 (over z, x).
Axes of the slice: x: 4, y: 4, z: 4, core: 2. Of those that a mesh axis runs over, the one named last changes fastest.
Arguments:
- particles: bfloat16 [8192, 256, 256], P(('stack', 'cls')), may hold values from -64 to 64
- classes: int32 [8192], P(('stack', 'cls')), may hold values from 0 to 511, as said below
- angles: int32 [8192], P(('stack', 'cls')), may hold values from 0 to 15
- groups: int32 [8192], P(('stack', 'cls')), may hold values from 0 to 15
- posterior: bfloat16 [8192, 2], P(('stack', 'cls')), may hold values from 0.099609375 to 1
- left_maps: bfloat16 [16, 256, 256], replicated, may hold values from -0.375 to 0.375
- right_maps: bfloat16 [16, 256, 256], replicated, may hold values from -0.375 to 0.375
- ctf_table: float32 [16, 256, 256], replicated, may hold values from -1 to 1
Outputs:
- class_sums: float32 [512, 256, 256], P('cls', 'stack')
- class_weights: float32 [512, 256, 256], P('cls', 'stack')
- class_norms: float32 [512], P('cls')
Inputs may be any that keep to these rules, and one draw needn't show every extreme that they name: Owner k holds classes k * 32 to (k + 1) * 32 - 1. Among the particles of one device at most 8 belong to one owner's classes; some owner gets exactly 8 from every device.
All inputs are finite; a program needn't handle non-finite values.
Results may differ from a plain program's by a relative error of at most 0.0029.
Values may be sent and summed in bfloat16 or wider, within the bound.
A program may use at most 192 MiB of HBM per device.

v0:
```python
import jax
import jax.numpy as jnp
from jax import lax
from jax.sharding import PartitionSpec as P

CLS_LOC = 32
CAP = 8


def rotate_block(block_images, weights_in, labels, left_maps, right_maps, ctf_table):
    angle_count = left_maps.shape[0]
    combined = None
    for nearby in range(weights_in.shape[1]):
        turn_now = (labels[:, 1] + nearby) % angle_count
        sheared = jnp.einsum(
            "bij,bkj->bik", block_images, right_maps[turn_now], preferred_element_type=jnp.float32
        ).astype(jnp.bfloat16)
        rotated = jnp.einsum(
            "bij,bjk->bik", left_maps[turn_now], sheared, preferred_element_type=jnp.float32
        )
        term = weights_in[:, nearby].astype(jnp.float32)[:, None, None] * rotated
        combined = term if combined is None else combined + term
    contrast = ctf_table[labels[:, 2]]
    return (contrast * combined, contrast)


def per_device(particles, classes, angles, groups, posterior, left_maps, right_maps, ctf_table):
    owners = lax.axis_size("cls")
    local_count = particles.shape[0]
    side = particles.shape[1]
    slot_count = owners * CAP
    owner_of = classes // CLS_LOC
    ordinal = jnp.arange(local_count, dtype=jnp.int32)
    matching = owner_of[:, None] == owner_of[None, :]
    ranking = jnp.sum((matching & (ordinal[None, :] < ordinal[:, None])).astype(jnp.int32), 1)
    slot_of = owner_of * CAP + ranking
    slot_hits = slot_of[None, :] == jnp.arange(slot_count, dtype=jnp.int32)[:, None]
    filled = jnp.any(slot_hits, 1)
    source = jnp.sum(jnp.where(slot_hits, ordinal[None, :], 0), 1)
    images = jnp.where(filled[:, None, None], particles[source], jnp.zeros((), jnp.bfloat16))
    weights_in = jnp.where(filled[:, None], posterior[source], jnp.zeros((), jnp.bfloat16))
    labels = jnp.stack(
        [classes[source] % CLS_LOC, angles[source], groups[source], filled.astype(jnp.int32)], 1
    )
    labels = jnp.where(filled[:, None], labels, 0)
    got_images, got_weights, got_labels = (
        lax.all_to_all(images, "cls", split_axis=0, concat_axis=0, tiled=True),
        lax.all_to_all(weights_in, "cls", split_axis=0, concat_axis=0, tiled=True),
        lax.all_to_all(labels, "cls", split_axis=0, concat_axis=0, tiled=True),
    )
    block_size = 16
    class_ids = jnp.arange(CLS_LOC, dtype=jnp.int32)

    def accumulate(totals, picked):
        block_images = got_images[picked]
        block_weights = got_weights[picked]
        block_labels = got_labels[picked]
        weighted, contrast = rotate_block(
            block_images, block_weights, block_labels, left_maps, right_maps, ctf_table
        )
        live = block_labels[:, 3] == 1
        onehot = ((block_labels[:, 0][:, None] == class_ids[None, :]) & live[:, None]).astype(
            jnp.float32
        )
        class_total = totals[0] + jnp.einsum(
            "bk,bij->kij", onehot, weighted, precision=lax.Precision.HIGHEST
        )
        power = jnp.mean(weighted * weighted, axis=(1, 2))
        power_total = totals[2] + jnp.dot(onehot.T, power, precision=lax.Precision.HIGHEST)
        posterior_sum = jnp.sum(block_weights.astype(jnp.float32), 1)
        second = totals[1] + jnp.einsum(
            "bk,bij->kij",
            onehot * posterior_sum[:, None],
            contrast * contrast,
            precision=lax.Precision.HIGHEST,
        )
        return (class_total, second, power_total)

    zero_images = jnp.zeros((CLS_LOC, side, side), jnp.float32)
    initial = (zero_images, zero_images, jnp.zeros((CLS_LOC,), jnp.float32))
    base_ids = jnp.arange(block_size, dtype=jnp.int32)

    def every_step(position, totals):
        return accumulate(totals, position * block_size + base_ids)

    totals = lax.fori_loop(0, slot_count // block_size, every_step, initial)
    class_sums, class_weights = (
        lax.psum_scatter(totals[0], "stack", scatter_dimension=1, tiled=True),
        lax.psum_scatter(totals[1], "stack", scatter_dimension=1, tiled=True),
    )
    class_norms = lax.psum(totals[2], "stack")
    return (class_sums, class_weights, class_norms)


def solution(mesh):
    return jax.shard_map(
        per_device,
        mesh=mesh,
        in_specs=(
            P(("stack", "cls"), None, None),
            P(("stack", "cls")),
            P(("stack", "cls")),
            P(("stack", "cls")),
            P(("stack", "cls"), None),
            P(),
            P(),
            P(),
        ),
        out_specs=(P("cls", "stack", None), P("cls", "stack", None), P("cls")),
        check_vma=False,
    )
```

profile of v0, /device:TPU:1, one launch (start us, length us, event | category | flops | bytes accessed | tf_op | source)
XLA Modules:
  0.0 954.1 jit_solution(10670407662504426535)
XLA Ops:
  11.3 8.4 all-to-all-start.1
  25.2 11.4 %gather_fusion.12 = bf16[128,256,256]{2,1,0:T(8,128)(2,1)} fusion(bf16[64,256,256]{2,1,0:T(8,128)(2,1)} %param.10, s32[1024]{0:T(1024)S(1)} %pad_clamp_fusion.4), kind=kCustom, calls=%fused_computation.12 | custom fusion | bytes 33554944 | tf_op jit(solution)/shard_map/gather | solution.py:40
  36.6 6.7 all-to-all-start
  43.2 14.0 %broadcast_select_fusion.1 = bf16[128,256,256]{2,1,0:T(8,128)(2,1)} fusion(bf16[128,256,256]{2,1,0:T(8,128)(2,1)} %gather_fusion.12, pred[128]{0:T(512)(128)(4,1)S(1)} %fusion.47), kind=kLoop, calls=%fused_computation.78 | loop fusion | flops 8388608 | bytes 33554560 | tf_op jit(solution)/shard_map/jit(_where)/select_n | solution.py:40
  57.2 6.8 all-to-all-start.2
  64.7 242.4 %all-to-all-done.2 = bf16[128,256,256]{2,1,0:T(8,128)(2,1)} async-done(((bf16[128,256,256]{2,1,0:T(8,128)(2,1)}), bf16[128,256,256]{2,1,0:T(8,128)(2,1)}, u32[]{:S(2)}, u32[]{:S(2)}) %all-to-all-start.2) | async-done | bytes 16777248 | tf_op jit(solution)/shard_map/all_to_all | solution.py:47
  307.1 518.1 %while.21 = (s32[]{:T(128)}, f32[32,256,256]{2,0,1:T(8,128)}, f32[32,256,256]{2,0,1:T(8,128)}, f32[32]{0:T(128)S(1)}, s32[128,4]{1,0:T(8,128)S(1)}, /*index=5*/f...) while((s32[]{:T(128)}, f32[32,256,256]{2,0,1:T(8,128)}, ...), condition=%wide.region_6.7_spmd.clone.clone, body=%wide.region_3.6_spmd.clone.clone.sunk | while | flops 2970630144 | bytes 138432032 | solution.py:86
  313.7 6.4 gather_fusion.3
  338.6 8.4 multiply_reduce_fusion.2
  347.1 10.3 %select_add_fusion.4 = f32[32,256,256]{2,0,1:T(8,128)} fusion(f32[32,256,256]{2,0,1:T(8,128)} %get-tuple-element.538, pred[]{:T(512)S(6)} %compare.15, f32[16,256,256]{2,1,0:T(8,128)} %get-tuple-element.521, s32[16]{0:T(128)S(1)} %get-tuple-element.522, pred[16]{0:T(512)(128)(4,1)S(1)} %fusion.89), kind=kOutput, calls=%fused_computation.16.clone.1 | convolution fusion | flops 406848512 | bytes 20971600 | tf_op jit(solution)/shard_map/while/body/eval_jaxpr/bk,bij->kij/dot_general | solution.py:65
  358.3 10.8 %select_add_fusion.5 = f32[32,256,256]{2,0,1:T(8,128)} fusion(f32[32,256,256]{2,0,1:T(8,128)} %get-tuple-element.539, pred[]{:T(512)S(6)} %compare.15, f32[16,256,256]{2,1,0:T(8,128)S(1)} %mul.172, f32[16]{0:T(128)S(1)} %convert_reduce_fusion.7, s32[16]{0:T(128)S(1)} %get-tuple-element.522, pred[16]{0:T(512)(128)(4,1)S(1)} %fusion.89), kind=kOutput, calls=%fused_computation.15.clone.1 | convolution fusion | flops 406849024 | bytes 20971664 | tf_op jit(solution)/shard_map/while/body/eval_jaxpr/bk,bij->kij/dot_general | solution.py:71
  375.7 6.4 gather_fusion.3
  400.6 8.4 multiply_reduce_fusion.2
  409.2 11.5 %select_add_fusion.4 = f32[32,256,256]{2,0,1:T(8,128)} fusion(f32[32,256,256]{2,0,1:T(8,128)} %get-tuple-element.538, pred[]{:T(512)S(6)} %compare.15, f32[16,256,256]{2,1,0:T(8,128)} %get-tuple-element.521, s32[16]{0:T(128)S(1)} %get-tuple-element.522, pred[16]{0:T(512)(128)(4,1)S(1)} %fusion.89), kind=kOutput, calls=%fused_computation.16.clone.1 | convolution fusion | flops 406848512 | bytes 20971600 | tf_op jit(solution)/shard_map/while/body/eval_jaxpr/bk,bij->kij/dot_general | solution.py:65
  421.6 12.7 %select_add_fusion.5 = f32[32,256,256]{2,0,1:T(8,128)} fusion(f32[32,256,256]{2,0,1:T(8,128)} %get-tuple-element.539, pred[]{:T(512)S(6)} %compare.15, f32[16,256,256]{2,1,0:T(8,128)S(1)} %mul.172, f32[16]{0:T(128)S(1)} %convert_reduce_fusion.7, s32[16]{0:T(128)S(1)} %get-tuple-element.522, pred[16]{0:T(512)(128)(4,1)S(1)} %fusion.89), kind=kOutput, calls=%fused_computation.15.clone.1 | convolution fusion | flops 406849024 | bytes 20971664 | tf_op jit(solution)/shard_map/while/body/eval_jaxpr/bk,bij->kij/dot_general | solution.py:71
  440.9 6.4 gather_fusion.3
  447.3 5.5 fusion.88
  465.8 8.4 multiply_reduce_fusion.2
  474.3 11.5 %select_add_fusion.4 = f32[32,256,256]{2,0,1:T(8,128)} fusion(f32[32,256,256]{2,0,1:T(8,128)} %get-tuple-element.538, pred[]{:T(512)S(6)} %compare.15, f32[16,256,256]{2,1,0:T(8,128)} %get-tuple-element.521, s32[16]{0:T(128)S(1)} %get-tuple-element.522, pred[16]{0:T(512)(128)(4,1)S(1)} %fusion.89), kind=kOutput, calls=%fused_computation.16.clone.1 | convolution fusion | flops 406848512 | bytes 20971600 | tf_op jit(solution)/shard_map/while/body/eval_jaxpr/bk,bij->kij/dot_general | solution.py:65
  486.7 12.7 %select_add_fusion.5 = f32[32,256,256]{2,0,1:T(8,128)} fusion(f32[32,256,256]{2,0,1:T(8,128)} %get-tuple-element.539, pred[]{:T(512)S(6)} %compare.15, f32[16,256,256]{2,1,0:T(8,128)S(1)} %mul.172, f32[16]{0:T(128)S(1)} %convert_reduce_fusion.7, s32[16]{0:T(128)S(1)} %get-tuple-element.522, pred[16]{0:T(512)(128)(4,1)S(1)} %fusion.89), kind=kOutput, calls=%fused_computation.15.clone.1 | convolution fusion | flops 406849024 | bytes 20971664 | tf_op jit(solution)/shard_map/while/body/eval_jaxpr/bk,bij->kij/dot_general | solution.py:71
  506.0 6.4 gather_fusion.3
  512.5 5.5 fusion.88
  530.9 8.4 multiply_reduce_fusion.2
  539.5 11.5 %select_add_fusion.4 = f32[32,256,256]{2,0,1:T(8,128)} fusion(f32[32,256,256]{2,0,1:T(8,128)} %get-tuple-element.538, pred[]{:T(512)S(6)} %compare.15, f32[16,256,256]{2,1,0:T(8,128)} %get-tuple-element.521, s32[16]{0:T(128)S(1)} %get-tuple-element.522, pred[16]{0:T(512)(128)(4,1)S(1)} %fusion.89), kind=kOutput, calls=%fused_computation.16.clone.1 | convolution fusion | flops 406848512 | bytes 20971600 | tf_op jit(solution)/shard_map/while/body/eval_jaxpr/bk,bij->kij/dot_general | solution.py:65
  551.9 12.7 %select_add_fusion.5 = f32[32,256,256]{2,0,1:T(8,128)} fusion(f32[32,256,256]{2,0,1:T(8,128)} %get-tuple-element.539, pred[]{:T(512)S(6)} %compare.15, f32[16,256,256]{2,1,0:T(8,128)S(1)} %mul.172, f32[16]{0:T(128)S(1)} %convert_reduce_fusion.7, s32[16]{0:T(128)S(1)} %get-tuple-element.522, pred[16]{0:T(512)(128)(4,1)S(1)} %fusion.89), kind=kOutput, calls=%fused_computation.15.clone.1 | convolution fusion | flops 406849024 | bytes 20971664 | tf_op jit(solution)/shard_map/while/body/eval_jaxpr/bk,bij->kij/dot_general | solution.py:71
  571.2 6.4 gather_fusion.3
  577.7 5.5 fusion.88
  596.1 8.4 multiply_reduce_fusion.2
  604.6 11.5 %select_add_fusion.4 = f32[32,256,256]{2,0,1:T(8,128)} fusion(f32[32,256,256]{2,0,1:T(8,128)} %get-tuple-element.538, pred[]{:T(512)S(6)} %compare.15, f32[16,256,256]{2,1,0:T(8,128)} %get-tuple-element.521, s32[16]{0:T(128)S(1)} %get-tuple-element.522, pred[16]{0:T(512)(128)(4,1)S(1)} %fusion.89), kind=kOutput, calls=%fused_computation.16.clone.1 | convolution fusion | flops 406848512 | bytes 20971600 | tf_op jit(solution)/shard_map/while/body/eval_jaxpr/bk,bij->kij/dot_general | solution.py:65
  617.0 12.7 %select_add_fusion.5 = f32[32,256,256]{2,0,1:T(8,128)} fusion(f32[32,256,256]{2,0,1:T(8,128)} %get-tuple-element.539, pred[]{:T(512)S(6)} %compare.15, f32[16,256,256]{2,1,0:T(8,128)S(1)} %mul.172, f32[16]{0:T(128)S(1)} %convert_reduce_fusion.7, s32[16]{0:T(128)S(1)} %get-tuple-element.522, pred[16]{0:T(512)(128)(4,1)S(1)} %fusion.89), kind=kOutput, calls=%fused_computation.15.clone.1 | convolution fusion | flops 406849024 | bytes 20971664 | tf_op jit(solution)/shard_map/while/body/eval_jaxpr/bk,bij->kij/dot_general | solution.py:71
  636.4 6.4 gather_fusion.3
  642.8 5.5 fusion.88
  661.2 8.4 multiply_reduce_fusion.2
  669.8 11.5 %select_add_fusion.4 = f32[32,256,256]{2,0,1:T(8,128)} fusion(f32[32,256,256]{2,0,1:T(8,128)} %get-tuple-element.538, pred[]{:T(512)S(6)} %compare.15, f32[16,256,256]{2,1,0:T(8,128)} %get-tuple-element.521, s32[16]{0:T(128)S(1)} %get-tuple-element.522, pred[16]{0:T(512)(128)(4,1)S(1)} %fusion.89), kind=kOutput, calls=%fused_computation.16.clone.1 | convolution fusion | flops 406848512 | bytes 20971600 | tf_op jit(solution)/shard_map/while/body/eval_jaxpr/bk,bij->kij/dot_general | solution.py:65
  682.2 12.7 %select_add_fusion.5 = f32[32,256,256]{2,0,1:T(8,128)} fusion(f32[32,256,256]{2,0,1:T(8,128)} %get-tuple-element.539, pred[]{:T(512)S(6)} %compare.15, f32[16,256,256]{2,1,0:T(8,128)S(1)} %mul.172, f32[16]{0:T(128)S(1)} %convert_reduce_fusion.7, s32[16]{0:T(128)S(1)} %get-tuple-element.522, pred[16]{0:T(512)(128)(4,1)S(1)} %fusion.89), kind=kOutput, calls=%fused_computation.15.clone.1 | convolution fusion | flops 406849024 | bytes 20971664 | tf_op jit(solution)/shard_map/while/body/eval_jaxpr/bk,bij->kij/dot_general | solution.py:71
  701.5 6.4 gather_fusion.3
  726.4 8.4 multiply_reduce_fusion.2
  734.9 11.5 %select_add_fusion.4 = f32[32,256,256]{2,0,1:T(8,128)} fusion(f32[32,256,256]{2,0,1:T(8,128)} %get-tuple-element.538, pred[]{:T(512)S(6)} %compare.15, f32[16,256,256]{2,1,0:T(8,128)} %get-tuple-element.521, s32[16]{0:T(128)S(1)} %get-tuple-element.522, pred[16]{0:T(512)(128)(4,1)S(1)} %fusion.89), kind=kOutput, calls=%fused_computation.16.clone.1 | convolution fusion | flops 406848512 | bytes 20971600 | tf_op jit(solution)/shard_map/while/body/eval_jaxpr/bk,bij->kij/dot_general | solution.py:65
  747.4 12.7 %select_add_fusion.5 = f32[32,256,256]{2,0,1:T(8,128)} fusion(f32[32,256,256]{2,0,1:T(8,128)} %get-tuple-element.539, pred[]{:T(512)S(6)} %compare.15, f32[16,256,256]{2,1,0:T(8,128)S(1)} %mul.172, f32[16]{0:T(128)S(1)} %convert_reduce_fusion.7, s32[16]{0:T(128)S(1)} %get-tuple-element.522, pred[16]{0:T(512)(128)(4,1)S(1)} %fusion.89), kind=kOutput, calls=%fused_computation.15.clone.1 | convolution fusion | flops 406849024 | bytes 20971664 | tf_op jit(solution)/shard_map/while/body/eval_jaxpr/bk,bij->kij/dot_general | solution.py:71
  766.7 6.4 gather_fusion.3
  791.5 8.4 multiply_reduce_fusion.2
  800.1 11.5 %select_add_fusion.4 = f32[32,256,256]{2,0,1:T(8,128)} fusion(f32[32,256,256]{2,0,1:T(8,128)} %get-tuple-element.538, pred[]{:T(512)S(6)} %compare.15, f32[16,256,256]{2,1,0:T(8,128)} %get-tuple-element.521, s32[16]{0:T(128)S(1)} %get-tuple-element.522, pred[16]{0:T(512)(128)(4,1)S(1)} %fusion.89), kind=kOutput, calls=%fused_computation.16.clone.1 | convolution fusion | flops 406848512 | bytes 20971600 | tf_op jit(solution)/shard_map/while/body/eval_jaxpr/bk,bij->kij/dot_general | solution.py:65
  812.5 12.7 %select_add_fusion.5 = f32[32,256,256]{2,0,1:T(8,128)} fusion(f32[32,256,256]{2,0,1:T(8,128)} %get-tuple-element.539, pred[]{:T(512)S(6)} %compare.15, f32[16,256,256]{2,1,0:T(8,128)S(1)} %mul.172, f32[16]{0:T(128)S(1)} %convert_reduce_fusion.7, s32[16]{0:T(128)S(1)} %get-tuple-element.522, pred[16]{0:T(512)(128)(4,1)S(1)} %fusion.89), kind=kOutput, calls=%fused_computation.15.clone.1 | convolution fusion | flops 406849024 | bytes 20971664 | tf_op jit(solution)/shard_map/while/body/eval_jaxpr/bk,bij->kij/dot_general | solution.py:71
  825.2 11.5 %copy.67 = f32[32,256,256]{2,1,0:T(8,128)} copy(f32[32,256,256]{2,0,1:T(8,128)} %get-tuple-element.566) | data formatting | bytes 16777216 | tf_op jit(solution)/shard_map/while | solution.py:86
  836.7 11.4 %copy.68 = f32[32,256,256]{2,1,0:T(8,128)} copy(f32[32,256,256]{2,0,1:T(8,128)} %get-tuple-element.567) | data formatting | bytes 16777216 | tf_op jit(solution)/shard_map/while | solution.py:86
  848.2 16.0 %psum.7 = f32[32]{0:T(128)} all-reduce(f32[32]{0:T(128)S(1)} %get-tuple-element.568), channel_id=1, replica_groups=mesh['stack'=8,'cls'=16] {'stack'}, use_global_device_ids=true, to_apply=%region_9.10 | all-reduce | flops 32 | bytes 256 | tf_op jit(solution)/shard_map/psum | solution.py:91
  864.2 28.0 %reduce-scatter.3.cloned.1.call-done = f32[32,32,256]{2,1,0:T(8,128)} async-done(((f32[32,256,256]{2,1,0:T(8,128)}), f32[32,32,256]{2,1,0:T(8,128)}) %reduce-scatter.3.cloned.1.call-update) | async-done | bytes 1048592 | tf_op jit(solution)/shard_map/reduce_scatter | solution.py:88
  892.2 55.1 %reduce-scatter.5.cloned.1.call-done = f32[32,32,256]{2,1,0:T(8,128)} async-done(((f32[32,256,256]{2,1,0:T(8,128)}), f32[32,32,256]{2,1,0:T(8,128)}) %reduce-scatter.5.cloned.1.call-update) | async-done | bytes 1048592 | tf_op jit(solution)/shard_map/reduce_scatter | solution.py:89
  (228 shorter events, 196.9 us)
Async XLA Ops:
  7.2 14.3 %copy-start = (s32[64]{0:T(128)S(1)}, s32[64]{0:T(128)}, u32[]{:S(2)}) copy-start(s32[64]{0:T(128)} %param.12) | copy-start | bytes 772
  11.3 25.3 %all-to-all-start.1 = ((bf16[16,8,2]{1,2,0:T(2,128)(2,1)}), bf16[16,8,2]{1,2,0:T(2,128)(2,1)S(1)}, u32[]{:S(2)}, u32[]{:S(2)}) async-start(bf16[16,8,2]{1,2,0:T(2,128)(2,1)} %broadcast_select_fusion.2), calls=%async_computation.1 | async-start | bytes 16384 | tf_op jit(solution)/shard_map/all_to_all | solution.py:48
  36.6 20.7 %all-to-all-start = ((s32[16,8,4]{1,2,0:T(4,128)}), s32[16,8,4]{1,2,0:T(4,128)S(1)}, u32[]{:S(2)}, u32[]{:S(2)}) async-start(s32[16,8,4]{1,2,0:T(4,128)} %copy.60), calls=%async_computation | async-start | bytes 65536 | tf_op jit(solution)/shard_map/all_to_all | solution.py:49
  57.2 249.9 %copy-start.3 = (bf16[16,256,256]{2,1,0:T(8,128)(2,1)S(1)}, bf16[16,256,256]{2,1,0:T(8,128)(2,1)}, u32[]{:S(2)}) copy-start(bf16[16,256,256]{2,1,0:T(8,128)(2,1)} %param.15) | copy-start | bytes 6291460
  57.2 249.9 %all-to-all-start.2 = ((bf16[128,256,256]{2,1,0:T(8,128)(2,1)}), bf16[128,256,256]{2,1,0:T(8,128)(2,1)}, u32[]{:S(2)}, u32[]{:S(2)}) async-start(bf16[128,256,256]{2,1,0:T(8,128)(2,1)} %broadcast_select_fusion.1), calls=%async_computation.2 | async-start | bytes 33554432 | tf_op jit(solution)/shard_map/all_to_all | solution.py:47
  64.1 828.1 %reduce-scatter.3.cloned.1.call-start = ((), (), s32[]{:S(2)}) async-start(), calls=%async_computation.5 | async-start | bytes 9437184 | tf_op jit(solution)/shard_map/reduce_scatter | solution.py:88
  347.1 10.4 %copy-start.2 = (f32[16,256,256]{2,1,0:T(8,128)S(1)}, f32[16,256,256]{2,1,0:T(8,128)}, u32[]{:S(2)}) copy-start(f32[16,256,256]{2,1,0:T(8,128)} %gather_fusion.1) | copy-start | bytes 12582916 | tf_op jit(solution)/shard_map/while
  358.3 10.8 %copy-start.4 = (bf16[16,256,256]{2,1,0:T(8,128)(2,1)S(1)}, bf16[16,256,256]{2,1,0:T(8,128)(2,1)}, u32[]{:S(2)}) copy-start(bf16[16,256,256]{2,1,0:T(8,128)(2,1)} %get-tuple-element.578) | copy-start | bytes 6291460 | tf_op jit(solution)/shard_map/while
  409.2 11.7 %copy-start.2 = (f32[16,256,256]{2,1,0:T(8,128)S(1)}, f32[16,256,256]{2,1,0:T(8,128)}, u32[]{:S(2)}) copy-start(f32[16,256,256]{2,1,0:T(8,128)} %gather_fusion.1) | copy-start | bytes 12582916 | tf_op jit(solution)/shard_map/while
  421.6 12.7 %copy-start.4 = (bf16[16,256,256]{2,1,0:T(8,128)(2,1)S(1)}, bf16[16,256,256]{2,1,0:T(8,128)(2,1)}, u32[]{:S(2)}) copy-start(bf16[16,256,256]{2,1,0:T(8,128)(2,1)} %get-tuple-element.578) | copy-start | bytes 6291460 | tf_op jit(solution)/shard_map/while
  474.3 11.7 %copy-start.2 = (f32[16,256,256]{2,1,0:T(8,128)S(1)}, f32[16,256,256]{2,1,0:T(8,128)}, u32[]{:S(2)}) copy-start(f32[16,256,256]{2,1,0:T(8,128)} %gather_fusion.1) | copy-start | bytes 12582916 | tf_op jit(solution)/shard_map/while
  486.7 12.7 %copy-start.4 = (bf16[16,256,256]{2,1,0:T(8,128)(2,1)S(1)}, bf16[16,256,256]{2,1,0:T(8,128)(2,1)}, u32[]{:S(2)}) copy-start(bf16[16,256,256]{2,1,0:T(8,128)(2,1)} %get-tuple-element.578) | copy-start | bytes 6291460 | tf_op jit(solution)/shard_map/while
  539.5 11.7 %copy-start.2 = (f32[16,256,256]{2,1,0:T(8,128)S(1)}, f32[16,256,256]{2,1,0:T(8,128)}, u32[]{:S(2)}) copy-start(f32[16,256,256]{2,1,0:T(8,128)} %gather_fusion.1) | copy-start | bytes 12582916 | tf_op jit(solution)/shard_map/while
  551.9 12.7 %copy-start.4 = (bf16[16,256,256]{2,1,0:T(8,128)(2,1)S(1)}, bf16[16,256,256]{2,1,0:T(8,128)(2,1)}, u32[]{:S(2)}) copy-start(bf16[16,256,256]{2,1,0:T(8,128)(2,1)} %get-tuple-element.578) | copy-start | bytes 6291460 | tf_op jit(solution)/shard_map/while
  604.6 11.7 %copy-start.2 = (f32[16,256,256]{2,1,0:T(8,128)S(1)}, f32[16,256,256]{2,1,0:T(8,128)}, u32[]{:S(2)}) copy-start(f32[16,256,256]{2,1,0:T(8,128)} %gather_fusion.1) | copy-start | bytes 12582916 | tf_op jit(solution)/shard_map/while
  617.0 12.7 %copy-start.4 = (bf16[16,256,256]{2,1,0:T(8,128)(2,1)S(1)}, bf16[16,256,256]{2,1,0:T(8,128)(2,1)}, u32[]{:S(2)}) copy-start(bf16[16,256,256]{2,1,0:T(8,128)(2,1)} %get-tuple-element.578) | copy-start | bytes 6291460 | tf_op jit(solution)/shard_map/while
  669.8 11.7 %copy-start.2 = (f32[16,256,256]{2,1,0:T(8,128)S(1)}, f32[16,256,256]{2,1,0:T(8,128)}, u32[]{:S(2)}) copy-start(f32[16,256,256]{2,1,0:T(8,128)} %gather_fusion.1) | copy-start | bytes 12582916 | tf_op jit(solution)/shard_map/while
  682.2 12.7 %copy-start.4 = (bf16[16,256,256]{2,1,0:T(8,128)(2,1)S(1)}, bf16[16,256,256]{2,1,0:T(8,128)(2,1)}, u32[]{:S(2)}) copy-start(bf16[16,256,256]{2,1,0:T(8,128)(2,1)} %get-tuple-element.578) | copy-start | bytes 6291460 | tf_op jit(solution)/shard_map/while
  734.9 11.7 %copy-start.2 = (f32[16,256,256]{2,1,0:T(8,128)S(1)}, f32[16,256,256]{2,1,0:T(8,128)}, u32[]{:S(2)}) copy-start(f32[16,256,256]{2,1,0:T(8,128)} %gather_fusion.1) | copy-start | bytes 12582916 | tf_op jit(solution)/shard_map/while
  747.4 12.7 %copy-start.4 = (bf16[16,256,256]{2,1,0:T(8,128)(2,1)S(1)}, bf16[16,256,256]{2,1,0:T(8,128)(2,1)}, u32[]{:S(2)}) copy-start(bf16[16,256,256]{2,1,0:T(8,128)(2,1)} %get-tuple-element.578) | copy-start | bytes 6291460 | tf_op jit(solution)/shard_map/while
  800.1 11.7 %copy-start.2 = (f32[16,256,256]{2,1,0:T(8,128)S(1)}, f32[16,256,256]{2,1,0:T(8,128)}, u32[]{:S(2)}) copy-start(f32[16,256,256]{2,1,0:T(8,128)} %gather_fusion.1) | copy-start | bytes 12582916 | tf_op jit(solution)/shard_map/while
  812.5 12.7 %copy-start.4 = (bf16[16,256,256]{2,1,0:T(8,128)(2,1)S(1)}, bf16[16,256,256]{2,1,0:T(8,128)(2,1)}, u32[]{:S(2)}) copy-start(bf16[16,256,256]{2,1,0:T(8,128)(2,1)} %get-tuple-element.578) | copy-start | bytes 6291460 | tf_op jit(solution)/shard_map/while
  836.7 110.6 %reduce-scatter.5.cloned.1.call-start = ((), (), s32[]{:S(2)}) async-start(), calls=%async_computation.6 | async-start | bytes 9437184 | tf_op jit(solution)/shard_map/reduce_scatter | solution.py:89
  848.2 99.1 %copy-start.1 = (s32[64]{0:T(128)S(1)}, s32[64]{0:T(128)}, u32[]{:S(2)}) copy-start(s32[64]{0:T(128)} %param.12) | copy-start | bytes 772
Sparse Core Ops, SparseCore 0:
  836.8 55.3 reduce-scatter.2
  895.1 52.0 reduce-scatter.4
where the time goes:
time: 956 us; the launch traced here: 954 us
  waiting for transfers between devices  326 us (34%)
  matrix products  302 us (32%)
  local copies, waits for them, and re-layouts  245 us (26%)
  other arithmetic  28.3 us (3%)
  starting transfers between devices  22.2 us (2%)
  blocking collectives  16 us (2%)
  between operations  14.2 us (1%)
    all_to_all x1, waiting for transfers between devices, per_device(): lax.all_to_all(images, 'cls', split_axis=0, concat_axis=0, tiled=True)  242 us
    dot_general x16, matrix products, rotate_block(): jnp.einsum('bij,bjk->bik', left_maps[turn_now], sheared, preferred_elemen...  111 us
    dot_general x8, matrix products, accumulate(): jnp.einsum('bk,bij->kij', onehot * posterior_sum[:, None], contrast * con...  99.5 us
    dot_general x8, matrix products, accumulate(): jnp.einsum('bk,bij->kij', onehot, weighted, precision=lax.Precision.HIGHEST)  90.9 us
    gather x16, local copies, waits for them, and re-layouts, rotate_block(): right_maps[turn_now]  57 us
    reduce_scatter x1, waiting for transfers between devices, per_device(): lax.psum_scatter(totals[1], 'stack', scatter_dimension=1, tiled=True)  55.1 us
    gather x8, local copies, waits for them, and re-layouts, accumulate(): block_images = got_images[picked]  51.6 us
    gather x16, local copies, waits for them, and re-layouts, rotate_block(): left_maps[turn_now]  45.6 us
  transfers between devices with their start and end apart: 5, of which 3 were waited for; matrix products, arithmetic and copies ran while one was open for 4% of the time, Pallas kernels for 0%

commit v1 on v0

v1 whole, which is shorter than its diff:
```python
import jax
import jax.numpy as jnp
from jax import lax
from jax.experimental import pallas as pl
from jax.experimental.pallas import tpu as pltpu
from jax.sharding import PartitionSpec as P

MESH = pl.DeviceIdType.MESH
F32 = jnp.float32
BF16 = jnp.bfloat16
SIDE = 256
ANGLES = 16
GROUPS = 16
LOCAL = 64
BATCH = 16
BATCHES = LOCAL // BATCH
STACK = 8
OWNERS = 16
CLS_LOC = 32
CLASSES = OWNERS * CLS_LOC
ROWS = SIDE // STACK
PEOPLE = STACK * LOCAL
PITCH = SIDE + 8
LANES = 128
CHUNKS = (8, 8, 4, 4, 4, 2, 2)
STARTS = tuple(sum(CHUNKS[:n]) for n in range(len(CHUNKS)))
NCHUNK = len(CHUNKS)
STACK_STEPS = tuple((dy, dc) for dy in (2, 1, 3, 0) for dc in (0, 1) if (dy, dc) != (0, 0))
NT = (((1,), (1,)), ((), ()))


def body(
    angles, groups, posterior, tile, particles, left_hbm, right_hbm, ctf_hbm,
    sums_out, weights_out, norms_out,
    left, right, ctf, images, weighted, power, outgoing, gathered,
    hot_a, hot_b, mixed, tiles, norm_tile, norm_tiles,
    partial, first_in, second, second_in,
    small, small_first, small_mid, small_second,
    load_sem, image_sem, own_sem,
    tile_send, tile_recv, norm_send, norm_recv,
    early_send, early_recv, y_send, y_recv,
    first_send, first_recv, second_send, second_recv,
    small_send, small_recv,
):
    s = lax.axis_index("stack")
    k = lax.axis_index("cls")
    y, core = s // 2, s % 2
    z, x = k // 4, k % 4

    def along_stack(step):
        return (((y + step[0]) % 4) * 2 + (core + step[1]) % 2, k)

    def along_x(d):
        return (s, z * 4 + (x + d) % 4)

    def along_z(d):
        return (s, ((z + d) % 4) * 4 + x)

    loads = [
        pltpu.make_async_copy(left_hbm, left, load_sem.at[0]),
        pltpu.make_async_copy(right_hbm, right, load_sem.at[1]),
        pltpu.make_async_copy(ctf_hbm, ctf, load_sem.at[2]),
    ]

    def image_load(b):
        return pltpu.make_async_copy(
            particles.at[pl.ds(b * BATCH, BATCH)], images.at[b % 2], image_sem.at[b % 2]
        )

    loads[1].start()
    image_load(0).start()
    loads[0].start()
    loads[2].start()
    image_load(1).start()

    barrier = pltpu.get_barrier_semaphore()
    peers = [along_stack(step) for step in STACK_STEPS]
    peers += [along_x(d) for d in (1, 2, 3)] + [along_z(d) for d in (1, 2, 3)]
    for peer in peers:
        pl.semaphore_signal(barrier, inc=1, device_id=peer, device_id_type=MESH)

    def remote(src, dst, send, recv, peer):
        return pltpu.make_async_remote_copy(
            src_ref=src, dst_ref=dst, send_sem=send, recv_sem=recv, device_id=peer, device_id_type=MESH
        )

    def tile_copies():
        return [
            remote(tile, tiles.at[s], tile_send.at[n], tile_recv.at[n], along_stack(step))
            for n, step in enumerate(STACK_STEPS)
        ]

    def norm_copies():
        return [
            remote(norm_tile, norm_tiles.at[s], norm_send.at[n], norm_recv.at[n], along_stack(step))
            for n, step in enumerate(STACK_STEPS)
        ]

    def early_copies(b):
        rows = CHUNKS[0]
        out = []
        for n, step in enumerate(STACK_STEPS):
            peer = along_stack(step)
            out.append(
                remote(
                    outgoing.at[pl.ds(peer[0] * ROWS, rows), pl.ds(b * BATCH, BATCH)],
                    gathered.at[pl.ds(0, rows), pl.ds(s * LOCAL + b * BATCH, BATCH)],
                    early_send.at[b, n], early_recv.at[b, n], peer,
                )
            )
        return out

    def y_copies(c):
        start, rows = STARTS[c], CHUNKS[c]
        out = []
        for n, step in enumerate(STACK_STEPS):
            peer = along_stack(step)
            out.append(
                remote(
                    outgoing.at[pl.ds(peer[0] * ROWS + start, rows)],
                    gathered.at[pl.ds(start, rows), pl.ds(s * LOCAL, LOCAL)],
                    y_send.at[c, n], y_recv.at[c, n], peer,
                )
            )
        return out

    def own_copy(c):
        start, rows = STARTS[c], CHUNKS[c]
        return pltpu.make_async_copy(
            outgoing.at[pl.ds(s * ROWS + start, rows)],
            gathered.at[pl.ds(start, rows), pl.ds(s * LOCAL, LOCAL)],
            own_sem.at[c],
        )

    def first_copies(c):
        half = CHUNKS[c] // 2
        out = []
        for d in (1, 2, 3):
            for part, (hop, spot) in enumerate(((along_x, (x + d) % 4), (along_z, (z + d) % 4))):
                rows = pl.ds(STARTS[c] + part * half, half)
                out.append(
                    remote(
                        partial.at[rows, pl.ds(spot * 128, 128)], first_in.at[d - 1, rows],
                        first_send.at[c, part, d - 1], first_recv.at[c, part, d - 1], hop(d),
                    )
                )
        return out

    def second_copies(c):
        half = CHUNKS[c] // 2
        out = []
        for d in (1, 2, 3):
            for part, (hop, spot) in enumerate(((along_z, (z + d) % 4), (along_x, (x + d) % 4))):
                rows = pl.ds(STARTS[c] + part * half, half)
                out.append(
                    remote(
                        second.at[rows, pl.ds(spot * CLS_LOC, CLS_LOC)], second_in.at[d - 1, rows],
                        second_send.at[c, part, d - 1], second_recv.at[c, part, d - 1], hop(d),
                    )
                )
        return out

    def small_first_copies():
        return [
            remote(
                small.at[pl.ds(((x + d) % 4) * 128, 128)], small_first.at[d - 1],
                small_send.at[0, d - 1], small_recv.at[0, d - 1], along_x(d),
            )
            for d in (1, 2, 3)
        ]

    def small_second_copies():
        return [
            remote(
                small_mid.at[pl.ds(((z + d) % 4) * CLS_LOC, CLS_LOC)], small_second.at[d - 1],
                small_send.at[1, d - 1], small_recv.at[1, d - 1], along_z(d),
            )
            for d in (1, 2, 3)
        ]

    def start(copies):
        for copy in copies:
            copy.start()

    def arrive(copies):
        for copy in copies:
            copy.wait_recv()

    def leave(copies):
        for copy in copies:
            copy.wait_send()

    for b in range(BATCHES):
        if b == 0:
            loads[1].wait()
        image_load(b).wait()
        if b == 0:
            loads[0].wait()
            loads[2].wait()

        def one(i, carry, b=b):
            p = b * BATCH + i
            turn = angles[p]
            after = (turn + 1) & (ANGLES - 1)
            image = images[b % 2, i]
            low = lax.dot_general(image, right[turn], NT, preferred_element_type=F32).astype(BF16)
            high = lax.dot_general(image, right[after], NT, preferred_element_type=F32).astype(BF16)
            spun = posterior[2 * p] * jnp.dot(left[turn], low, preferred_element_type=F32)
            spun += posterior[2 * p + 1] * jnp.dot(left[after], high, preferred_element_type=F32)
            spun = ctf[groups[p]] * spun
            weighted[0, pl.ds(i * PITCH, SIDE), :] = spun[:, :LANES]
            weighted[1, pl.ds(i * PITCH, SIDE), :] = spun[:, LANES:]
            squares = jnp.sum(spun * spun, axis=0, keepdims=True)
            power[pl.ds(p, 1), :] = squares[:, :LANES] + squares[:, LANES:]
            return carry

        lax.fori_loop(0, BATCH, one, 0)
        if b + 2 < BATCHES:
            image_load(b + 2).start()

        def turn_over(r, carry, b=b):
            for h in range(2):
                lines = weighted[h, pl.ds(r, BATCH, stride=PITCH), :]
                outgoing[r, b * BATCH:(b + 1) * BATCH, h * LANES:(h + 1) * LANES] = lines.astype(BF16)
            return carry

        lax.fori_loop(0, SIDE, turn_over, 0, unroll=8)
        if b == 0:
            pl.semaphore_wait(barrier, len(peers))
            start(tile_copies())
        start(early_copies(b))

    start(y_copies(1))
    for c in range(NCHUNK):
        own_copy(c).start()

    tiles[s] = tile[...]
    lane = lax.broadcasted_iota(jnp.int32, (8, LANES), 1)
    own_power = jnp.sum(power[...], axis=1, keepdims=True) * (1.0 / (SIDE * SIDE))
    spot = lax.broadcasted_iota(jnp.int32, (LOCAL, LANES), 1) & (LOCAL - 1)
    line = lax.broadcasted_iota(jnp.int32, (LOCAL, LANES), 0)
    own_power = jnp.sum(jnp.where(spot == line, own_power, 0.0), axis=0, keepdims=True)
    norm_tile[...] = jnp.broadcast_to(own_power, (8, LANES))
    norm_tiles[s] = jnp.broadcast_to(own_power, (8, LANES))
    start(norm_copies())

    arrive(tile_copies())
    q = lax.broadcasted_iota(jnp.int32, (CLASSES, LANES), 0)
    swapped = (((q >> 5) & 3) * 4 + (q >> 7)) * CLS_LOC + (q & (CLS_LOC - 1))
    natural = q.astype(F32)
    swapped = swapped.astype(F32)
    which = lax.broadcasted_iota(jnp.int32, (LANES, LANES), 0)
    which_group = (which & (GROUPS - 1)).astype(F32)
    for j in range(STACK // 2):
        cols = slice(j * LANES, (j + 1) * LANES)
        both = jnp.where(lane < LOCAL, tiles[2 * j], tiles[2 * j + 1])
        hot_a[:, cols] = jnp.where(swapped == both[0:1], 1.0, 0.0).astype(BF16)
        hot_b[:, cols] = jnp.where(natural == both[0:1], 1.0, 0.0).astype(BF16)
        chance = jnp.where(which < GROUPS, both[2:3], both[3:4])
        keep = (which_group == both[1:2]) & (which < 2 * GROUPS)
        mixed[:, cols] = jnp.where(keep, chance, 0.0).astype(BF16)

    def small_start():
        arrive(norm_copies())
        total = jnp.zeros((CLASSES, LANES), F32)
        for j in range(STACK // 2):
            both = jnp.where(lane < LOCAL, tiles[2 * j], tiles[2 * j + 1])
            norm = jnp.where(lane < LOCAL, norm_tiles[2 * j], norm_tiles[2 * j + 1])
            total += jnp.where(swapped == both[0:1], norm[0:1], 0.0)
        small[:, 0:LANES] = total
        small[:, LANES:2 * LANES] = lax.dot_general(hot_a[...], mixed[...], NT, preferred_element_type=F32)
        start(small_first_copies())

    def small_middle():
        arrive(small_first_copies())
        small_mid[...] = (
            small[pl.ds(x * 128, 128), :] + small_first[0] + small_first[1] + small_first[2]
        )
        start(small_second_copies())

    def small_end():
        arrive(small_second_copies())
        total = small_mid[pl.ds(z * CLS_LOC, CLS_LOC), :] + small_second[0] + small_second[1] + small_second[2]
        norms = jnp.sum(total[:, :LANES], axis=1, keepdims=True)
        norms_out[...] = jnp.broadcast_to(norms, (CLS_LOC, LANES))
        coef = total[:, LANES:LANES + GROUPS] + total[:, LANES + GROUPS:LANES + 2 * GROUPS]

        def weigh(r, carry):
            lines = jnp.concatenate([ctf[g, pl.ds(s * ROWS + r, 1), :] for g in range(GROUPS)], axis=0)
            weights_out[r] = jnp.dot(
                coef, lines * lines, precision=lax.Precision.HIGHEST, preferred_element_type=F32
            )
            return carry

        lax.fori_loop(0, ROWS, weigh, 0)

    def by_class(c):
        half = CHUNKS[c] // 2
        for part, hot in enumerate((hot_a, hot_b)):

            def add(i, carry, part=part, hot=hot):
                r = STARTS[c] + part * half + i
                partial[r] = jnp.dot(hot[...], gathered[r], preferred_element_type=F32).astype(BF16)
                return carry

            lax.fori_loop(0, half, add, 0)

    def add_first(c):
        half = CHUNKS[c] // 2
        for part, mine in enumerate((x, z)):

            def add(i, carry, part=part, mine=mine):
                r = STARTS[c] + part * half + i
                total = partial[r, pl.ds(mine * 128, 128), :].astype(F32)
                for d in range(3):
                    total += first_in[d, r].astype(F32)
                second[r] = total
                return carry

            lax.fori_loop(0, half, add, 0)

    def add_second(c):
        half = CHUNKS[c] // 2
        for part, mine in enumerate((z, x)):

            def add(i, carry, part=part, mine=mine):
                r = STARTS[c] + part * half + i
                total = second[r, pl.ds(mine * CLS_LOC, CLS_LOC), :]
                for d in range(3):
                    total += second_in[d, r]
                sums_out[r] = total
                return carry

            lax.fori_loop(0, half, add, 0)

    for step in range(NCHUNK + 2):
        c = step
        if c + 2 < NCHUNK:
            start(y_copies(c + 2))
        if c < NCHUNK:
            if c == 0:
                for b in range(BATCHES):
                    arrive(early_copies(b))
            else:
                arrive(y_copies(c))
            own_copy(c).wait()
            by_class(c)
            start(first_copies(c))
        if c == 0:
            small_start()
        if c == 1:
            small_middle()
        if 0 <= c - 1 < NCHUNK:
            arrive(first_copies(c - 1))
            add_first(c - 1)
            start(second_copies(c - 1))
        if c == 2:
            small_end()
        if 0 <= c - 2 < NCHUNK:
            arrive(second_copies(c - 2))
            add_second(c - 2)

    leave(tile_copies())
    leave(norm_copies())
    for b in range(BATCHES):
        leave(early_copies(b))
    for c in range(NCHUNK):
        if c > 0:
            leave(y_copies(c))
        leave(first_copies(c))
        leave(second_copies(c))
    leave(small_first_copies())
    leave(small_second_copies())


def per_device(particles, classes, angles, groups, posterior, left_maps, right_maps, ctf_table):
    chances = posterior.astype(F32)
    tile = jnp.stack([classes.astype(F32), groups.astype(F32), chances[:, 0], chances[:, 1]], 0)
    tile = jnp.pad(jnp.concatenate([tile, tile], 1), ((0, 4), (0, 0)))
    smem = pl.BlockSpec(memory_space=pltpu.SMEM)
    vmem = pl.BlockSpec(memory_space=pltpu.VMEM)
    hbm = pl.BlockSpec(memory_space=pl.ANY)
    n = len(STACK_STEPS)
    dma = pltpu.SemaphoreType.DMA
    sums, weights, norms = pl.pallas_call(
        body,
        out_shape=(
            jax.ShapeDtypeStruct((ROWS, CLS_LOC, SIDE), F32),
            jax.ShapeDtypeStruct((ROWS, CLS_LOC, SIDE), F32),
            jax.ShapeDtypeStruct((CLS_LOC, LANES), F32),
        ),
        in_specs=[smem, smem, smem, vmem, hbm, hbm, hbm, hbm],
        out_specs=(vmem, vmem, vmem),
        scratch_shapes=[
            pltpu.VMEM((ANGLES, SIDE, SIDE), BF16),
            pltpu.VMEM((ANGLES, SIDE, SIDE), BF16),
            pltpu.VMEM((GROUPS, SIDE, SIDE), F32),
            pltpu.VMEM((2, BATCH, SIDE, SIDE), BF16),
            pltpu.VMEM((2, BATCH * PITCH, LANES), F32),
            pltpu.VMEM((LOCAL, LANES), F32),
            pltpu.VMEM((SIDE, LOCAL, SIDE), BF16),
            pltpu.VMEM((ROWS, PEOPLE, SIDE), BF16),
            pltpu.VMEM((CLASSES, PEOPLE), BF16),
            pltpu.VMEM((CLASSES, PEOPLE), BF16),
            pltpu.VMEM((LANES, PEOPLE), BF16),
            pltpu.VMEM((STACK, 8, LANES), F32),
            pltpu.VMEM((8, LANES), F32),
            pltpu.VMEM((STACK, 8, LANES), F32),
            pltpu.VMEM((ROWS, CLASSES, SIDE), BF16),
            pltpu.VMEM((3, ROWS, 128, SIDE), BF16),
            pltpu.VMEM((ROWS, 128, SIDE), F32),
            pltpu.VMEM((3, ROWS, CLS_LOC, SIDE), F32),
            pltpu.VMEM((CLASSES, 2 * LANES), F32),
            pltpu.VMEM((3, 128, 2 * LANES), F32),
            pltpu.VMEM((128, 2 * LANES), F32),
            pltpu.VMEM((3, CLS_LOC, 2 * LANES), F32),
            dma((3,)), dma((2,)), dma((NCHUNK,)),
            dma((n,)), dma((n,)), dma((n,)), dma((n,)),
            dma((BATCHES, n)), dma((BATCHES, n)), dma((NCHUNK, n)), dma((NCHUNK, n)),
            dma((NCHUNK, 2, 3)), dma((NCHUNK, 2, 3)), dma((NCHUNK, 2, 3)), dma((NCHUNK, 2, 3)),
            dma((2, 3)), dma((2, 3)),
        ],
        compiler_params=pltpu.CompilerParams(
            collective_id=0, has_side_effects=True, vmem_limit_bytes=63 * 1024 * 1024
        ),
        name="class_sums",
    )(angles, groups, chances.reshape(-1), tile, particles, left_maps, right_maps, ctf_table)
    return (jnp.transpose(sums, (1, 0, 2)), jnp.transpose(weights, (1, 0, 2)), norms[:, 0])


def solution(mesh):
    return jax.shard_map(
        per_device,
        mesh=mesh,
        in_specs=(
            P(("stack", "cls"), None, None),
            P(("stack", "cls")),
            P(("stack", "cls")),
            P(("stack", "cls")),
            P(("stack", "cls"), None),
            P(),
            P(),
            P(),
        ),
        out_specs=(P("cls", "stack", None), P("cls", "stack", None), P("cls")),
        check_vma=False,
    )
```

time: 956 us -> 158 us (0.17)
  waiting for transfers between devices: 326 us -> 0 us
  matrix products: 302 us -> 0 us
  local copies, waits for them, and re-layouts: 245 us -> 7.65 us
  Pallas kernels: 0 us -> 147 us
  other arithmetic: 28.3 us -> 2.01 us
  starting transfers between devices: 22.2 us -> 0 us
  blocking collectives: 16 us -> 0 us
  between operations: 14.2 us -> 0.65 us
    dot_general x40 -> x0, matrix products: 302 us -> none  [the longest x16 111 us: rotate_block(): jnp.einsum('bij,bjk->bik', left_maps[turn_now], sheared, preferred_elemen...]
    all_to_all x3 -> x0, waiting for transfers between devices: 242 us -> none  [the longest x1 242 us: per_device(): lax.all_to_all(images, 'cls', split_axis=0, concat_axis=0, tiled=True)]
    gather x71 -> x0, local copies, waits for them, and re-layouts: 219 us -> none  [the longest x16 57 us: rotate_block(): right_maps[turn_now]]
    pallas_call x0 -> x1, Pallas kernels: none -> 147 us  [per_device(): pl.pallas_call(body, out_shape=(jax.ShapeDtypeStruct((ROWS, CLS_LOC, SIDE...]
    reduce_scatter x2 -> x0, waiting for transfers between devices: 83.1 us -> none  [the longest x1 55.1 us: per_device(): lax.psum_scatter(totals[1], 'stack', scatter_dimension=1, tiled=True)]
    while x34 -> x0, local copies, waits for them, and re-layouts: 23 us -> none  [the longest x2 22.9 us: per_device(): totals = lax.fori_loop(0, slot_count // block_size, every_step, initial)]
    all_to_all x3 -> x0, starting transfers between devices: 21.9 us -> none  [the longest x1 8.43 us: per_device(): lax.all_to_all(weights_in, 'cls', split_axis=0, concat_axis=0, tiled=True)]
    select_n x14 -> x0, other arithmetic: 16.2 us -> none  [the longest x1 14 us: per_device(): jnp.where(filled[:, None, None], particles[source], jnp.zeros((), jnp.bfl...]
  transfers between devices with their start and end apart: 5 -> 0, of which waited for: 3 -> 0; matrix products, arithmetic and copies ran while one was open for 4% -> 0% of each run, Pallas kernels for 0% -> 0%
where the time goes in v1:
time: 158 us; the launch traced here: 157 us
  Pallas kernels  147 us (93%)
  local copies, waits for them, and re-layouts  7.65 us (5%)
  other arithmetic  2.01 us (1%)
    pallas_call x1, Pallas kernels, per_device(): pl.pallas_call(body, out_shape=(jax.ShapeDtypeStruct((ROWS, CLS_LOC, SIDE...  147 us
    unnamed x4, local copies, waits for them, and re-layouts  5.62 us

profile of v1, /device:TPU:1, one launch (start us, length us, event | category | flops | bytes accessed | tf_op | source)
XLA Modules:
  0.0 157.1 jit_solution(3415740555472114766)
XLA Ops:
  0.6 0.7 convert_element_type.11
  1.3 0.7 convert_bitcast_fusion
  2.0 0.7 fusion.tile
  2.6 0.8 copy.14
  3.4 0.7 reshape.9.posterior
  4.0 146.8 %class_sums.1 = (f32[32,32,256]{2,1,0:T(8,128)}, f32[32,32,256]{2,1,0:T(8,128)}, f32[32,128]{1,0:T(8,128)}) custom-call(s32[64]{0:T(128)} %angles.1, s32[64]{0:T(128)} %groups.1, f32[128]{0:T(128)} %reshape.9.posterior, f32[8,128]{1,0:T(8,128)} %fusion.tile, bf16[64,256,256]{2,1,0:T(8,128)(2,1)} %particles.1, bf16[16,256,256]{2,1,0:T(8,128)(2,1)} %left_hbm.1, ...), custom_call_target="tpu_custom_call" | custom-call | tf_op jit(solution)/shard_map/class_sums/pallas_call | solution.py:385
  150.8 0.0 copy-start
  150.8 2.8 %copy.15 = f32[32,32,256]{2,1,0:T(8,128)} copy(f32[32,32,256]{2,0,1:T(8,128)} %bitcast.11) | data formatting | bytes 2097152
  153.6 2.8 %copy.16 = f32[32,32,256]{2,1,0:T(8,128)} copy(f32[32,32,256]{2,0,1:T(8,128)} %bitcast.10) | data formatting | bytes 2097152
  156.4 0.0 copy-done
  156.4 0.6 slice_reduce_fusion
  (1 shorter events, 0.0 us)
Async XLA Ops:
  150.8 5.6 %copy-start = (f32[32,128]{1,0:T(8,128)S(1)}, f32[32,128]{1,0:T(8,128)}, u32[]{:S(2)}) copy-start(f32[32,128]{1,0:T(8,128)} %get-tuple-element.8) | copy-start | bytes 49156

commit v2 on v1

--- a/solution.py
+++ b/solution.py
@@ -21,26 +21,30 @@
 ROWS = SIDE // STACK
 PEOPLE = STACK * LOCAL
 PITCH = SIDE + 8
+TOGETHER = 8
 LANES = 128
-CHUNKS = (8, 8, 4, 4, 4, 2, 2)
+CHUNKS = (6, 6, 4, 4, 4, 4, 2, 2)
 STARTS = tuple(sum(CHUNKS[:n]) for n in range(len(CHUNKS)))
 NCHUNK = len(CHUNKS)
+AHEAD = 2
+FIRST_LAG = 1
+SECOND_LAG = 2
 STACK_STEPS = tuple((dy, dc) for dy in (2, 1, 3, 0) for dc in (0, 1) if (dy, dc) != (0, 0))
 NT = (((1,), (1,)), ((), ()))
 
 
 def body(
-    angles, groups, posterior, tile, particles, left_hbm, right_hbm, ctf_hbm,
+    angles, groups, class_row, group_row, chance_rows, particles, left_hbm, right_hbm, ctf_hbm,
     sums_out, weights_out, norms_out,
     left, right, ctf, images, weighted, power, outgoing, gathered,
-    hot_a, hot_b, mixed, tiles, norm_tile, norm_tiles,
+    hot_a, hot_b, mixed, tile, posterior, tiles, norm_tile, norm_tiles,
     partial, first_in, second, second_in,
-    small, small_first, small_mid, small_second,
+    small, small_first, small_mid, small_second, staged,
     load_sem, image_sem, own_sem,
     tile_send, tile_recv, norm_send, norm_recv,
     early_send, early_recv, y_send, y_recv,
     first_send, first_recv, second_send, second_recv,
-    small_send, small_recv,
+    small_send, small_recv, result_sem,
 ):
     s = lax.axis_index("stack")
     k = lax.axis_index("cls")
@@ -72,6 +76,14 @@
     loads[0].start()
     loads[2].start()
     image_load(1).start()
+
+    labels = jnp.concatenate(
+        [class_row[...].astype(F32), group_row[...].astype(F32), chance_rows[...].astype(F32)], axis=0
+    )
+    tile[0:4, :] = jnp.concatenate([labels, labels], axis=1)
+    tile[4:8, :] = jnp.zeros((4, LANES), F32)
+    to_scalars = pltpu.make_async_copy(tile, posterior, load_sem.at[3])
+    to_scalars.start()
 
     barrier = pltpu.get_barrier_semaphore()
     peers = [along_stack(step) for step in STACK_STEPS]
@@ -104,7 +116,7 @@
             out.append(
                 remote(
                     outgoing.at[pl.ds(peer[0] * ROWS, rows), pl.ds(b * BATCH, BATCH)],
-                    gathered.at[pl.ds(0, rows), pl.ds(s * LOCAL + b * BATCH, BATCH)],
+                    gathered.at[s, pl.ds(0, rows), pl.ds(b * BATCH, BATCH)],
                     early_send.at[b, n], early_recv.at[b, n], peer,
                 )
             )
@@ -118,7 +130,7 @@
             out.append(
                 remote(
                     outgoing.at[pl.ds(peer[0] * ROWS + start, rows)],
-                    gathered.at[pl.ds(start, rows), pl.ds(s * LOCAL, LOCAL)],
+                    gathered.at[s, pl.ds(start, rows)],
                     y_send.at[c, n], y_recv.at[c, n], peer,
                 )
             )
@@ -128,7 +140,7 @@
         start, rows = STARTS[c], CHUNKS[c]
         return pltpu.make_async_copy(
             outgoing.at[pl.ds(s * ROWS + start, rows)],
-            gathered.at[pl.ds(start, rows), pl.ds(s * LOCAL, LOCAL)],
+            gathered.at[s, pl.ds(start, rows)],
             own_sem.at[c],
         )
 
@@ -140,7 +152,7 @@
                 rows = pl.ds(STARTS[c] + part * half, half)
                 out.append(
                     remote(
-                        partial.at[rows, pl.ds(spot * 128, 128)], first_in.at[d - 1, rows],
+                        partial.at[spot, rows], first_in.at[d - 1, rows],
                         first_send.at[c, part, d - 1], first_recv.at[c, part, d - 1], hop(d),
                     )
                 )
@@ -154,7 +166,7 @@
                 rows = pl.ds(STARTS[c] + part * half, half)
                 out.append(
                     remote(
-                        second.at[rows, pl.ds(spot * CLS_LOC, CLS_LOC)], second_in.at[d - 1, rows],
+                        second.at[spot, rows], second_in.at[d - 1, rows],
                         second_send.at[c, part, d - 1], second_recv.at[c, part, d - 1], hop(d),
                     )
                 )
@@ -197,24 +209,32 @@
         if b == 0:
             loads[0].wait()
             loads[2].wait()
-
-        def one(i, carry, b=b):
-            p = b * BATCH + i
-            turn = angles[p]
-            after = (turn + 1) & (ANGLES - 1)
-            image = images[b % 2, i]
-            low = lax.dot_general(image, right[turn], NT, preferred_element_type=F32).astype(BF16)
-            high = lax.dot_general(image, right[after], NT, preferred_element_type=F32).astype(BF16)
-            spun = posterior[2 * p] * jnp.dot(left[turn], low, preferred_element_type=F32)
-            spun += posterior[2 * p + 1] * jnp.dot(left[after], high, preferred_element_type=F32)
-            spun = ctf[groups[p]] * spun
-            weighted[0, pl.ds(i * PITCH, SIDE), :] = spun[:, :LANES]
-            weighted[1, pl.ds(i * PITCH, SIDE), :] = spun[:, LANES:]
-            squares = jnp.sum(spun * spun, axis=0, keepdims=True)
-            power[pl.ds(p, 1), :] = squares[:, :LANES] + squares[:, LANES:]
+            to_scalars.wait()
+
+        def several(n, carry, b=b):
+            spots = [n * TOGETHER + m for m in range(TOGETHER)]
+            turns, sheared = [], []
+            for i in spots:
+                turn = angles[b * BATCH + i]
+                turns.append((turn, (turn + 1) & (ANGLES - 1)))
+            for i, near in zip(spots, turns):
+                image = images[b % 2, i]
+                sheared.append([
+                    lax.dot_general(image, right[turn], NT, preferred_element_type=F32).astype(BF16)
+                    for turn in near
+                ])
+            for i, near, pair in zip(spots, turns, sheared):
+                p = b * BATCH + i
+                spun = posterior[2, p] * jnp.dot(left[near[0]], pair[0], preferred_element_type=F32)
+                spun += posterior[3, p] * jnp.dot(left[near[1]], pair[1], preferred_element_type=F32)
+                spun = ctf[groups[p]] * spun
+                weighted[0, pl.ds(i * PITCH, SIDE), :] = spun[:, :LANES]
+                weighted[1, pl.ds(i * PITCH, SIDE), :] = spun[:, LANES:]
+                squares = jnp.sum(spun * spun, axis=0, keepdims=True)
+                power[pl.ds(p, 1), :] = squares[:, :LANES] + squares[:, LANES:]
             return carry
 
-        lax.fori_loop(0, BATCH, one, 0)
+        lax.fori_loop(0, BATCH // TOGETHER, several, 0)
         if b + 2 < BATCHES:
             image_load(b + 2).start()
 
@@ -230,7 +250,8 @@
             start(tile_copies())
         start(early_copies(b))
 
-    start(y_copies(1))
+    for c in range(1, AHEAD):
+        start(y_copies(c))
     for c in range(NCHUNK):
         own_copy(c).start()
 
@@ -260,6 +281,28 @@
         keep = (which_group == both[1:2]) & (which < 2 * GROUPS)
         mixed[:, cols] = jnp.where(keep, chance, 0.0).astype(BF16)
 
+    def keep_lines(which, r, lines):
+        at = pl.ds((which * ROWS + r) * CLS_LOC, CLS_LOC)
+        weighted[0, at, :] = lines[:, :LANES]
+        weighted[1, at, :] = lines[:, LANES:]
+
+    def result_copy(which, block):
+        rows = pl.ds(block * 8, 8)
+        target = (sums_out, weights_out)[which]
+        return pltpu.make_async_copy(
+            staged.at[which, :, rows], target.at[:, rows], result_sem.at[which, block]
+        )
+
+    def settle(which, block):
+        def one_class(i, carry):
+            for h in range(2):
+                at = pl.ds((which * ROWS + block * 8) * CLS_LOC + i, 8, stride=CLS_LOC)
+                staged[which, i, block * 8:block * 8 + 8, h * LANES:(h + 1) * LANES] = weighted[h, at, :]
+            return carry
+
+        lax.fori_loop(0, CLS_LOC, one_class, 0, unroll=8)
+        result_copy(which, block).start()
+
     def small_start():
         arrive(norm_copies())
         total = jnp.zeros((CLASSES, LANES), F32)
@@ -287,12 +330,15 @@
 
         def weigh(r, carry):
             lines = jnp.concatenate([ctf[g, pl.ds(s * ROWS + r, 1), :] for g in range(GROUPS)], axis=0)
-            weights_out[r] = jnp.dot(
+            spread = jnp.dot(
                 coef, lines * lines, precision=lax.Precision.HIGHEST, preferred_element_type=F32
             )
+            keep_lines(1, r, spread)
             return carry
 
         lax.fori_loop(0, ROWS, weigh, 0)
+        for block in range(ROWS // 8):
+            settle(1, block)
 
     def by_class(c):
         half = CHUNKS[c] // 2
@@ -300,7 +346,9 @@
 
             def add(i, carry, part=part, hot=hot):
                 r = STARTS[c] + part * half + i
-                partial[r] = jnp.dot(hot[...], gathered[r], preferred_element_type=F32).astype(BF16)
+                lines = gathered[:, r].reshape(PEOPLE, SIDE)
+                sums = jnp.dot(hot[...], lines, preferred_element_type=F32).astype(BF16)
+                partial[:, r] = sums.reshape(4, 128, SIDE)
                 return carry
 
             lax.fori_loop(0, half, add, 0)
@@ -311,10 +359,10 @@
 
             def add(i, carry, part=part, mine=mine):
                 r = STARTS[c] + part * half + i
-                total = partial[r, pl.ds(mine * 128, 128), :].astype(F32)
+                total = partial[mine, r].astype(F32)
                 for d in range(3):
                     total += first_in[d, r].astype(F32)
-                second[r] = total
+                second[:, r] = total.reshape(4, CLS_LOC, SIDE)
                 return carry
 
             lax.fori_loop(0, half, add, 0)
@@ -325,24 +373,23 @@
 
             def add(i, carry, part=part, mine=mine):
                 r = STARTS[c] + part * half + i
-                total = second[r, pl.ds(mine * CLS_LOC, CLS_LOC), :]
+                total = second[mine, r]
                 for d in range(3):
                     total += second_in[d, r]
-                sums_out[r] = total
+                keep_lines(0, r, total)
                 return carry
 
             lax.fori_loop(0, half, add, 0)
 
-    for step in range(NCHUNK + 2):
-        c = step
-        if c + 2 < NCHUNK:
-            start(y_copies(c + 2))
+    for c in range(NCHUNK + SECOND_LAG):
         if c < NCHUNK:
             if c == 0:
                 for b in range(BATCHES):
                     arrive(early_copies(b))
             else:
                 arrive(y_copies(c))
+            if c + AHEAD < NCHUNK:
+                start(y_copies(c + AHEAD))
             own_copy(c).wait()
             by_class(c)
             start(first_copies(c))
@@ -350,15 +397,18 @@
             small_start()
         if c == 1:
             small_middle()
-        if 0 <= c - 1 < NCHUNK:
-            arrive(first_copies(c - 1))
-            add_first(c - 1)
-            start(second_copies(c - 1))
+        if 0 <= c - FIRST_LAG < NCHUNK:
+            arrive(first_copies(c - FIRST_LAG))
+            add_first(c - FIRST_LAG)
+            start(second_copies(c - FIRST_LAG))
         if c == 2:
             small_end()
-        if 0 <= c - 2 < NCHUNK:
-            arrive(second_copies(c - 2))
-            add_second(c - 2)
+        if 0 <= c - SECOND_LAG < NCHUNK:
+            arrive(second_copies(c - SECOND_LAG))
+            add_second(c - SECOND_LAG)
+            begun = STARTS[c - SECOND_LAG]
+            for block in range(begun // 8, (begun + CHUNKS[c - SECOND_LAG]) // 8):
+                settle(0, block)
 
     leave(tile_copies())
     leave(norm_copies())
@@ -371,12 +421,12 @@
         leave(second_copies(c))
     leave(small_first_copies())
     leave(small_second_copies())
+    for which in range(2):
+        for block in range(ROWS // 8):
+            result_copy(which, block).wait()
 
 
 def per_device(particles, classes, angles, groups, posterior, left_maps, right_maps, ctf_table):
-    chances = posterior.astype(F32)
-    tile = jnp.stack([classes.astype(F32), groups.astype(F32), chances[:, 0], chances[:, 1]], 0)
-    tile = jnp.pad(jnp.concatenate([tile, tile], 1), ((0, 4), (0, 0)))
     smem = pl.BlockSpec(memory_space=pltpu.SMEM)
     vmem = pl.BlockSpec(memory_space=pltpu.VMEM)
     hbm = pl.BlockSpec(memory_space=pl.ANY)
@@ -385,12 +435,12 @@
     sums, weights, norms = pl.pallas_call(
         body,
         out_shape=(
-            jax.ShapeDtypeStruct((ROWS, CLS_LOC, SIDE), F32),
-            jax.ShapeDtypeStruct((ROWS, CLS_LOC, SIDE), F32),
+            jax.ShapeDtypeStruct((CLS_LOC, ROWS, SIDE), F32),
+            jax.ShapeDtypeStruct((CLS_LOC, ROWS, SIDE), F32),
             jax.ShapeDtypeStruct((CLS_LOC, LANES), F32),
         ),
-        in_specs=[smem, smem, smem, vmem, hbm, hbm, hbm, hbm],
-        out_specs=(vmem, vmem, vmem),
+        in_specs=[smem, smem, vmem, vmem, vmem, hbm, hbm, hbm, hbm],
+        out_specs=(hbm, hbm, vmem),
         scratch_shapes=[
             pltpu.VMEM((ANGLES, SIDE, SIDE), BF16),
             pltpu.VMEM((ANGLES, SIDE, SIDE), BF16),
@@ -399,33 +449,36 @@
             pltpu.VMEM((2, BATCH * PITCH, LANES), F32),
             pltpu.VMEM((LOCAL, LANES), F32),
             pltpu.VMEM((SIDE, LOCAL, SIDE), BF16),
-            pltpu.VMEM((ROWS, PEOPLE, SIDE), BF16),
+            pltpu.VMEM((STACK, ROWS, LOCAL, SIDE), BF16),
             pltpu.VMEM((CLASSES, PEOPLE), BF16),
             pltpu.VMEM((CLASSES, PEOPLE), BF16),
             pltpu.VMEM((LANES, PEOPLE), BF16),
+            pltpu.VMEM((8, LANES), F32),
+            pltpu.SMEM((8, LANES), F32),
             pltpu.VMEM((STACK, 8, LANES), F32),
             pltpu.VMEM((8, LANES), F32),
             pltpu.VMEM((STACK, 8, LANES), F32),
-            pltpu.VMEM((ROWS, CLASSES, SIDE), BF16),
+            pltpu.VMEM((4, ROWS, 128, SIDE), BF16),
             pltpu.VMEM((3, ROWS, 128, SIDE), BF16),
-            pltpu.VMEM((ROWS, 128, SIDE), F32),
+            pltpu.VMEM((4, ROWS, CLS_LOC, SIDE), F32),
             pltpu.VMEM((3, ROWS, CLS_LOC, SIDE), F32),
             pltpu.VMEM((CLASSES, 2 * LANES), F32),
             pltpu.VMEM((3, 128, 2 * LANES), F32),
             pltpu.VMEM((128, 2 * LANES), F32),
             pltpu.VMEM((3, CLS_LOC, 2 * LANES), F32),
-            dma((3,)), dma((2,)), dma((NCHUNK,)),
+            pltpu.VMEM((2, CLS_LOC, ROWS, SIDE), F32),
+            dma((4,)), dma((2,)), dma((NCHUNK,)),
             dma((n,)), dma((n,)), dma((n,)), dma((n,)),
             dma((BATCHES, n)), dma((BATCHES, n)), dma((NCHUNK, n)), dma((NCHUNK, n)),
             dma((NCHUNK, 2, 3)), dma((NCHUNK, 2, 3)), dma((NCHUNK, 2, 3)), dma((NCHUNK, 2, 3)),
-            dma((2, 3)), dma((2, 3)),
+            dma((2, 3)), dma((2, 3)), dma((2, ROWS // 8)),
         ],
         compiler_params=pltpu.CompilerParams(
             collective_id=0, has_side_effects=True, vmem_limit_bytes=63 * 1024 * 1024
         ),
         name="class_sums",
-    )(angles, groups, chances.reshape(-1), tile, particles, left_maps, right_maps, ctf_table)
-    return (jnp.transpose(sums, (1, 0, 2)), jnp.transpose(weights, (1, 0, 2)), norms[:, 0])
+    )(angles, groups, classes.reshape(1, LOCAL), groups.reshape(1, LOCAL), posterior.T, particles, left_maps, right_maps, ctf_table)
+    return (sums, weights, norms[:, 0])
 
 
 def solution(mesh):

time: 158 us -> 134 us (0.85)
  Pallas kernels: 147 us -> 127 us
  other arithmetic: 2.01 us -> 0 us
  local copies, waits for them, and re-layouts: 7.65 us -> 5.96 us
    pallas_call x1, Pallas kernels: 147 us -> 127 us  [per_device(): pl.pallas_call(body, out_shape=(jax.ShapeDtypeStruct((CLS_LOC, ROWS, SIDE...]
    unnamed x4 -> x2, local copies, waits for them, and re-layouts: 5.62 us -> 4.61 us
where the time goes in v2:
time: 134 us
  Pallas kernels  127 us (95%)
  local copies, waits for them, and re-layouts  5.96 us (4%)
    pallas_call x1, Pallas kernels, per_device(): pl.pallas_call(body, out_shape=(jax.ShapeDtypeStruct((CLS_LOC, ROWS, SIDE...  127 us
    unnamed x2, local copies, waits for them, and re-layouts  4.61 us

profile of v2, /device:TPU:1, one launch (start us, length us, event | category | flops | bytes accessed | tf_op | source)
XLA Modules:
  0.0 134.0 jit_solution(10817657043192365219)
XLA Ops:
  0.6 127.4 %class_sums.1 = (f32[32,32,256]{2,1,0:T(8,128)}, f32[32,32,256]{2,1,0:T(8,128)}, f32[32,128]{1,0:T(8,128)}) custom-call(s32[64]{0:T(128)} %angles.1, s32[64]{0:T(128)} %groups.1, s32[1,64]{1,0:T(1,128)} %bitcast.4, s32[1,64]{1,0:T(1,128)} %bitcast.3, bf16[2,64]{1,0:T(2,128)(2,1)} %bitcast.5, bf16[64,256,256]{2,1,0:T(8,128)(2,1)} %particles.1, ...), custom_call_target="tpu_custom_call" | custom-call | tf_op jit(solution)/shard_map/class_sums/pallas_call | solution.py:435
  128.1 1.3 %slice_reduce_fusion = f32[32]{0:T(128)} fusion(f32[32,128]{1,0:T(8,128)} %get-tuple-element.8), kind=kLoop, calls=%fused_computation | loop fusion | bytes 256 | tf_op jit(solution)/shard_map/slice | solution.py:481
  129.4 2.3 %copy.13 = f32[32,32,256]{2,1,0:T(8,128)} copy(f32[32,32,256]{2,1,0:T(8,128)} %get-tuple-element.12) | data formatting | bytes 2097152
  131.7 2.3 %copy.14 = f32[32,32,256]{2,1,0:T(8,128)} copy(f32[32,32,256]{2,1,0:T(8,128)} %get-tuple-element.13) | data formatting | bytes 2097152

commit v3 on v2

--- a/solution.py
+++ b/solution.py
@@ -23,13 +23,18 @@
 PITCH = SIDE + 8
 TOGETHER = 8
 LANES = 128
-CHUNKS = (6, 6, 4, 4, 4, 4, 2, 2)
-STARTS = tuple(sum(CHUNKS[:n]) for n in range(len(CHUNKS)))
+CHUNKS = (4, 4, 4, 4, 4, 2, 2)
+SIDEWAYS = 8
+SIDES = 2
+STRAIGHT = ROWS - SIDEWAYS
+STARTS = tuple(SIDEWAYS + sum(CHUNKS[:n]) for n in range(len(CHUNKS)))
 NCHUNK = len(CHUNKS)
 AHEAD = 2
 FIRST_LAG = 1
 SECOND_LAG = 2
+SIDE_LAGS = (2, 4)
 STACK_STEPS = tuple((dy, dc) for dy in (2, 1, 3, 0) for dc in (0, 1) if (dy, dc) != (0, 0))
+ACROSS_STEPS = tuple((dx, dc) for dx in (2, 1, 3, 0) for dc in (0, 1) if (dx, dc) != (0, 0))
 NT = (((1,), (1,)), ((), ()))
 
 
@@ -37,14 +42,15 @@
     angles, groups, class_row, group_row, chance_rows, particles, left_hbm, right_hbm, ctf_hbm,
     sums_out, weights_out, norms_out,
     left, right, ctf, images, weighted, power, outgoing, gathered,
-    hot_a, hot_b, mixed, tile, posterior, tiles, norm_tile, norm_tiles,
+    hot, hot_x, mixed, tile, posterior, tiles, tiles_x, norm_tile, norm_tiles,
     partial, first_in, second, second_in,
-    small, small_first, small_mid, small_second, staged,
+    small, small_first, small_mid, small_second, staged, side_second_in, side_third, side_third_in,
     load_sem, image_sem, own_sem,
     tile_send, tile_recv, norm_send, norm_recv,
     early_send, early_recv, y_send, y_recv,
     first_send, first_recv, second_send, second_recv,
     small_send, small_recv, result_sem,
+    across_send, across_recv, tile_x_send, tile_x_recv, side_send, side_recv, side_own_sem,
 ):
     s = lax.axis_index("stack")
     k = lax.axis_index("cls")
@@ -54,11 +60,25 @@
     def along_stack(step):
         return (((y + step[0]) % 4) * 2 + (core + step[1]) % 2, k)
 
+    def across(side, step):
+        there = (z * 4 + (x + step[0]) % 4, ((z + step[0]) % 4) * 4 + x)[side]
+        return (y * 2 + (core + step[1]) % 2, there)
+
     def along_x(d):
         return (s, z * 4 + (x + d) % 4)
 
     def along_z(d):
         return (s, ((z + d) % 4) * 4 + x)
+
+    def along_y(d):
+        return (((y + d) % 4) * 2 + core, k)
+
+    wide, deep = (x, z), (z, x)
+    along_wide, along_deep = (along_x, along_z), (along_z, along_x)
+
+    def spread_at(side):
+        return wide[side] * 2 + core
+
 
     loads = [
         pltpu.make_async_copy(left_hbm, left, load_sem.at[0]),
@@ -87,6 +107,8 @@
 
     barrier = pltpu.get_barrier_semaphore()
     peers = [along_stack(step) for step in STACK_STEPS]
+    for side in range(SIDES):
+        peers += [across(side, step) for step in ACROSS_STEPS if step[0] != 0 and step[1] != 0]
     peers += [along_x(d) for d in (1, 2, 3)] + [along_z(d) for d in (1, 2, 3)]
     for peer in peers:
         pl.semaphore_signal(barrier, inc=1, device_id=peer, device_id_type=MESH)
@@ -102,11 +124,76 @@
             for n, step in enumerate(STACK_STEPS)
         ]
 
+    def tile_x_copies():
+        return [
+            remote(
+                tile, tiles_x.at[side, spread_at(side)],
+                tile_x_send.at[side, n], tile_x_recv.at[side, n], across(side, step),
+            )
+            for side in range(SIDES)
+            for n, step in enumerate(ACROSS_STEPS)
+        ]
+
+    def sideways(side, spot):
+        return side * STACK * 4 + spot * 4
+
+    def across_copies(b):
+        out = []
+        for n, step in enumerate(ACROSS_STEPS):
+            for side in range(SIDES):
+                spot = ((wide[side] + step[0]) % 4) * 2 + (core + step[1]) % 2
+                out.append(
+                    remote(
+                        outgoing.at[pl.ds(sideways(side, spot), 4), pl.ds(b * BATCH, BATCH)],
+                        gathered.at[spread_at(side), pl.ds(side * 4, 4), pl.ds(b * BATCH, BATCH)],
+                        across_send.at[b, side, n], across_recv.at[b, side, n], across(side, step),
+                    )
+                )
+        return out
+
+    def across_own(side):
+        return pltpu.make_async_copy(
+            outgoing.at[pl.ds(sideways(side, spread_at(side)), 4)],
+            gathered.at[spread_at(side), pl.ds(side * 4, 4)],
+            side_own_sem.at[side],
+        )
+
+    def side_first(side):
+        rows = pl.ds(side * 4, 4)
+        return [
+            remote(
+                partial.at[(deep[side] + d) % 4, rows], first_in.at[d - 1, rows],
+                side_send.at[side, 0, d - 1], side_recv.at[side, 0, d - 1], along_deep[side](d),
+            )
+            for d in (1, 2, 3)
+        ]
+
+    def side_second(side):
+        return [
+            remote(
+                second.at[:, pl.ds(side * 4 + (y + d) % 4, 1)], side_second_in.at[side, d - 1],
+                side_send.at[side, 1, d - 1], side_recv.at[side, 1, d - 1], along_y(d),
+            )
+            for d in (1, 2, 3)
+        ]
+
+    def side_last(side):
+        return [
+            remote(
+                side_third.at[side, (wide[side] + d) % 4], side_third_in.at[side, d - 1],
+                side_send.at[side, 2, d - 1], side_recv.at[side, 2, d - 1], along_wide[side](d),
+            )
+            for d in (1, 2, 3)
+        ]
+
     def norm_copies():
         return [
             remote(norm_tile, norm_tiles.at[s], norm_send.at[n], norm_recv.at[n], along_stack(step))
             for n, step in enumerate(STACK_STEPS)
         ]
+
+    def straight(block, row):
+        return STACK * SIDEWAYS + block * STRAIGHT + row - SIDEWAYS
 
     def early_copies(b):
         rows = CHUNKS[0]
@@ -115,8 +202,8 @@
             peer = along_stack(step)
             out.append(
                 remote(
-                    outgoing.at[pl.ds(peer[0] * ROWS, rows), pl.ds(b * BATCH, BATCH)],
-                    gathered.at[s, pl.ds(0, rows), pl.ds(b * BATCH, BATCH)],
+                    outgoing.at[pl.ds(straight(peer[0], STARTS[0]), rows), pl.ds(b * BATCH, BATCH)],
+                    gathered.at[s, pl.ds(STARTS[0], rows), pl.ds(b * BATCH, BATCH)],
                     early_send.at[b, n], early_recv.at[b, n], peer,
                 )
             )
@@ -129,7 +216,7 @@
             peer = along_stack(step)
             out.append(
                 remote(
-                    outgoing.at[pl.ds(peer[0] * ROWS + start, rows)],
+                    outgoing.at[pl.ds(straight(peer[0], start), rows)],
                     gathered.at[s, pl.ds(start, rows)],
                     y_send.at[c, n], y_recv.at[c, n], peer,
                 )
@@ -139,7 +226,7 @@
     def own_copy(c):
         start, rows = STARTS[c], CHUNKS[c]
         return pltpu.make_async_copy(
-            outgoing.at[pl.ds(s * ROWS + start, rows)],
+            outgoing.at[pl.ds(straight(s, start), rows)],
             gathered.at[s, pl.ds(start, rows)],
             own_sem.at[c],
         )
@@ -166,7 +253,7 @@
                 rows = pl.ds(STARTS[c] + part * half, half)
                 out.append(
                     remote(
-                        second.at[spot, rows], second_in.at[d - 1, rows],
+                        second.at[spot, rows], second_in.at[d - 1, pl.ds(STARTS[c] - SIDEWAYS + part * half, half)],
                         second_send.at[c, part, d - 1], second_recv.at[c, part, d - 1], hop(d),
                     )
                 )
@@ -238,16 +325,23 @@
         if b + 2 < BATCHES:
             image_load(b + 2).start()
 
-        def turn_over(r, carry, b=b):
-            for h in range(2):
-                lines = weighted[h, pl.ds(r, BATCH, stride=PITCH), :]
-                outgoing[r, b * BATCH:(b + 1) * BATCH, h * LANES:(h + 1) * LANES] = lines.astype(BF16)
+        def turn_over(block, carry, b=b):
+            for r in range(ROWS):
+                if r < SIDEWAYS:
+                    place = sideways(r // 4, (r % 4) * 2 + (block & 1)) + (block >> 1)
+                else:
+                    place = straight(block, r)
+                for h in range(2):
+                    lines = weighted[h, pl.ds(block * ROWS + r, BATCH, stride=PITCH), :]
+                    outgoing[place, b * BATCH:(b + 1) * BATCH, h * LANES:(h + 1) * LANES] = lines.astype(BF16)
             return carry
 
-        lax.fori_loop(0, SIDE, turn_over, 0, unroll=8)
+        lax.fori_loop(0, STACK, turn_over, 0)
         if b == 0:
             pl.semaphore_wait(barrier, len(peers))
             start(tile_copies())
+            start(tile_x_copies())
+        start(across_copies(b))
         start(early_copies(b))
 
     for c in range(1, AHEAD):
@@ -255,7 +349,12 @@
     for c in range(NCHUNK):
         own_copy(c).start()
 
+    for side in range(SIDES):
+        across_own(side).start()
+
     tiles[s] = tile[...]
+    for side in range(SIDES):
+        tiles_x[side, spread_at(side)] = tile[...]
     lane = lax.broadcasted_iota(jnp.int32, (8, LANES), 1)
     own_power = jnp.sum(power[...], axis=1, keepdims=True) * (1.0 / (SIDE * SIDE))
     spot = lax.broadcasted_iota(jnp.int32, (LOCAL, LANES), 1) & (LOCAL - 1)
@@ -266,23 +365,23 @@
     start(norm_copies())
 
     arrive(tile_copies())
-    q = lax.broadcasted_iota(jnp.int32, (CLASSES, LANES), 0)
-    swapped = (((q >> 5) & 3) * 4 + (q >> 7)) * CLS_LOC + (q & (CLS_LOC - 1))
-    natural = q.astype(F32)
-    swapped = swapped.astype(F32)
+    arrive(tile_x_copies())
+    natural = lax.broadcasted_iota(jnp.int32, (CLASSES, LANES), 0).astype(F32)
     which = lax.broadcasted_iota(jnp.int32, (LANES, LANES), 0)
     which_group = (which & (GROUPS - 1)).astype(F32)
     for j in range(STACK // 2):
         cols = slice(j * LANES, (j + 1) * LANES)
         both = jnp.where(lane < LOCAL, tiles[2 * j], tiles[2 * j + 1])
-        hot_a[:, cols] = jnp.where(swapped == both[0:1], 1.0, 0.0).astype(BF16)
-        hot_b[:, cols] = jnp.where(natural == both[0:1], 1.0, 0.0).astype(BF16)
+        hot[:, cols] = jnp.where(natural == both[0:1], 1.0, 0.0).astype(BF16)
+        for side in range(SIDES):
+            beside = jnp.where(lane < LOCAL, tiles_x[side, 2 * j], tiles_x[side, 2 * j + 1])
+            hot_x[side, :, cols] = jnp.where(natural == beside[0:1], 1.0, 0.0).astype(BF16)
         chance = jnp.where(which < GROUPS, both[2:3], both[3:4])
         keep = (which_group == both[1:2]) & (which < 2 * GROUPS)
         mixed[:, cols] = jnp.where(keep, chance, 0.0).astype(BF16)
 
     def keep_lines(which, r, lines):
-        at = pl.ds((which * ROWS + r) * CLS_LOC, CLS_LOC)
+        at = pl.ds(pl.multiple_of((which * ROWS + r) * CLS_LOC, CLS_LOC), CLS_LOC)
         weighted[0, at, :] = lines[:, :LANES]
         weighted[1, at, :] = lines[:, LANES:]
 
@@ -309,9 +408,12 @@
         for j in range(STACK // 2):
             both = jnp.where(lane < LOCAL, tiles[2 * j], tiles[2 * j + 1])
             norm = jnp.where(lane < LOCAL, norm_tiles[2 * j], norm_tiles[2 * j + 1])
-            total += jnp.where(swapped == both[0:1], norm[0:1], 0.0)
-        small[:, 0:LANES] = total
-        small[:, LANES:2 * LANES] = lax.dot_general(hot_a[...], mixed[...], NT, preferred_element_type=F32)
+            total += jnp.where(natural == both[0:1], norm[0:1], 0.0)
+        blend = lax.dot_general(hot[...], mixed[...], NT, preferred_element_type=F32)
+        for owner in range(OWNERS):
+            line = ((owner % 4) * 4 + owner // 4) * CLS_LOC
+            small[line:line + CLS_LOC, 0:LANES] = total[owner * CLS_LOC:(owner + 1) * CLS_LOC]
+            small[line:line + CLS_LOC, LANES:2 * LANES] = blend[owner * CLS_LOC:(owner + 1) * CLS_LOC]
         start(small_first_copies())
 
     def small_middle():
@@ -340,15 +442,24 @@
         for block in range(ROWS // 8):
             settle(1, block)
 
+    def keep_partial(part, r, sums):
+        if part == 0:
+            for owner in range(OWNERS):
+                line = (owner // 4) * CLS_LOC
+                block = sums[owner * CLS_LOC:(owner + 1) * CLS_LOC]
+                partial[owner % 4, r, line:line + CLS_LOC, :] = block
+        else:
+            partial[:, r] = sums.reshape(4, 128, SIDE)
+
     def by_class(c):
         half = CHUNKS[c] // 2
-        for part, hot in enumerate((hot_a, hot_b)):
-
-            def add(i, carry, part=part, hot=hot):
+        for part in range(2):
+
+            def add(i, carry, part=part):
                 r = STARTS[c] + part * half + i
                 lines = gathered[:, r].reshape(PEOPLE, SIDE)
                 sums = jnp.dot(hot[...], lines, preferred_element_type=F32).astype(BF16)
-                partial[:, r] = sums.reshape(4, 128, SIDE)
+                keep_partial(part, r, sums)
                 return carry
 
             lax.fori_loop(0, half, add, 0)
@@ -375,11 +486,44 @@
                 r = STARTS[c] + part * half + i
                 total = second[mine, r]
                 for d in range(3):
-                    total += second_in[d, r]
+                    total += second_in[d, r - SIDEWAYS]
                 keep_lines(0, r, total)
                 return carry
 
             lax.fori_loop(0, half, add, 0)
+
+    def side_by_class(side):
+        def add(i, carry):
+            r = side * 4 + i
+            lines = gathered[:, r].reshape(PEOPLE, SIDE)
+            sums = jnp.dot(hot_x[side], lines, preferred_element_type=F32).astype(BF16)
+            keep_partial(1 - side, r, sums)
+            return carry
+
+        lax.fori_loop(0, 4, add, 0)
+
+    def side_add_first(side):
+        def add(i, carry):
+            r = side * 4 + i
+            total = partial[deep[side], r].astype(F32)
+            for d in range(3):
+                total += first_in[d, r].astype(F32)
+            second[:, r] = total.reshape(4, CLS_LOC, SIDE)
+            return carry
+
+        lax.fori_loop(0, 4, add, 0)
+
+    def side_add_second(side):
+        for block in range(4):
+            total = second[block, side * 4 + y]
+            for d in range(3):
+                total += side_second_in[side, d, block, 0]
+            side_third[side, block] = total
+
+    def side_keep(side):
+        keep_lines(0, side * 4 + wide[side], side_third[side, wide[side]])
+        for d in (1, 2, 3):
+            keep_lines(0, side * 4 + (wide[side] + 4 - d) % 4, side_third_in[side, d - 1])
 
     for c in range(NCHUNK + SECOND_LAG):
         if c < NCHUNK:
@@ -393,6 +537,28 @@
             own_copy(c).wait()
             by_class(c)
             start(first_copies(c))
+        if c == 0:
+            for b in range(BATCHES):
+                arrive(across_copies(b))
+            for side in range(SIDES):
+                across_own(side).wait()
+                side_by_class(side)
+                start(side_first(side))
+        if c == SIDE_LAGS[0]:
+            for side in range(SIDES):
+                arrive(side_first(side))
+                side_add_first(side)
+                start(side_second(side))
+        if c == SIDE_LAGS[1]:
+            for side in range(SIDES):
+                arrive(side_second(side))
+                side_add_second(side)
+                start(side_last(side))
+        if c == NCHUNK:
+            for side in range(SIDES):
+                arrive(side_last(side))
+                side_keep(side)
+            settle(0, 0)
         if c == 0:
             small_start()
         if c == 1:
@@ -421,6 +587,13 @@
         leave(second_copies(c))
     leave(small_first_copies())
     leave(small_second_copies())
+    leave(tile_x_copies())
+    for b in range(BATCHES):
+        leave(across_copies(b))
+    for side in range(SIDES):
+        leave(side_first(side))
+        leave(side_second(side))
+        leave(side_last(side))
     for which in range(2):
         for block in range(ROWS // 8):
             result_copy(which, block).wait()
@@ -451,27 +624,33 @@
             pltpu.VMEM((SIDE, LOCAL, SIDE), BF16),
             pltpu.VMEM((STACK, ROWS, LOCAL, SIDE), BF16),
             pltpu.VMEM((CLASSES, PEOPLE), BF16),
-            pltpu.VMEM((CLASSES, PEOPLE), BF16),
+            pltpu.VMEM((SIDES, CLASSES, PEOPLE), BF16),
             pltpu.VMEM((LANES, PEOPLE), BF16),
             pltpu.VMEM((8, LANES), F32),
             pltpu.SMEM((8, LANES), F32),
             pltpu.VMEM((STACK, 8, LANES), F32),
+            pltpu.VMEM((SIDES, STACK, 8, LANES), F32),
             pltpu.VMEM((8, LANES), F32),
             pltpu.VMEM((STACK, 8, LANES), F32),
             pltpu.VMEM((4, ROWS, 128, SIDE), BF16),
             pltpu.VMEM((3, ROWS, 128, SIDE), BF16),
             pltpu.VMEM((4, ROWS, CLS_LOC, SIDE), F32),
-            pltpu.VMEM((3, ROWS, CLS_LOC, SIDE), F32),
+            pltpu.VMEM((3, STRAIGHT, CLS_LOC, SIDE), F32),
             pltpu.VMEM((CLASSES, 2 * LANES), F32),
             pltpu.VMEM((3, 128, 2 * LANES), F32),
             pltpu.VMEM((128, 2 * LANES), F32),
             pltpu.VMEM((3, CLS_LOC, 2 * LANES), F32),
             pltpu.VMEM((2, CLS_LOC, ROWS, SIDE), F32),
+            pltpu.VMEM((SIDES, 3, 4, 1, CLS_LOC, SIDE), F32),
+            pltpu.VMEM((SIDES, 4, CLS_LOC, SIDE), F32),
+            pltpu.VMEM((SIDES, 3, CLS_LOC, SIDE), F32),
             dma((4,)), dma((2,)), dma((NCHUNK,)),
             dma((n,)), dma((n,)), dma((n,)), dma((n,)),
             dma((BATCHES, n)), dma((BATCHES, n)), dma((NCHUNK, n)), dma((NCHUNK, n)),
             dma((NCHUNK, 2, 3)), dma((NCHUNK, 2, 3)), dma((NCHUNK, 2, 3)), dma((NCHUNK, 2, 3)),
             dma((2, 3)), dma((2, 3)), dma((2, ROWS // 8)),
+            dma((BATCHES, SIDES, n)), dma((BATCHES, SIDES, n)), dma((SIDES, n)), dma((SIDES, n)),
+            dma((SIDES, 3, 3)), dma((SIDES, 3, 3)), dma((SIDES,)),
         ],
         compiler_params=pltpu.CompilerParams(
             collective_id=0, has_side_effects=True, vmem_limit_bytes=63 * 1024 * 1024

time: 134 us -> 122 us (0.910)
  Pallas kernels: 127 us -> 115 us
    pallas_call x1, Pallas kernels: 127 us -> 115 us  [per_device(): pl.pallas_call(body, out_shape=(jax.ShapeDtypeStruct((CLS_LOC, ROWS, SIDE...]
where the time goes in v3:
time: 122 us
  Pallas kernels  115 us (94%)
  local copies, waits for them, and re-layouts  5.96 us (5%)
    pallas_call x1, Pallas kernels, per_device(): pl.pallas_call(body, out_shape=(jax.ShapeDtypeStruct((CLS_LOC, ROWS, SIDE...  115 us
    unnamed x2, local copies, waits for them, and re-layouts  4.61 us

profile of v3, /device:TPU:1, one launch (start us, length us, event | category | flops | bytes accessed | tf_op | source)
XLA Modules:
  0.0 122.1 jit_solution(12396844965215948499)
XLA Ops:
  0.6 115.5 %class_sums.1 = (f32[32,32,256]{2,1,0:T(8,128)}, f32[32,32,256]{2,1,0:T(8,128)}, f32[32,128]{1,0:T(8,128)}) custom-call(s32[64]{0:T(128)} %angles.1, s32[64]{0:T(128)} %groups.1, s32[1,64]{1,0:T(1,128)} %bitcast.4, s32[1,64]{1,0:T(1,128)} %bitcast.3, bf16[2,64]{1,0:T(2,128)(2,1)} %bitcast.5, bf16[64,256,256]{2,1,0:T(8,128)(2,1)} %particles.1, ...), custom_call_target="tpu_custom_call" | custom-call | tf_op jit(solution)/shard_map/class_sums/pallas_call | solution.py:608
  116.1 1.3 %slice_reduce_fusion = f32[32]{0:T(128)} fusion(f32[32,128]{1,0:T(8,128)} %get-tuple-element.8), kind=kLoop, calls=%fused_computation | loop fusion | bytes 256 | tf_op jit(solution)/shard_map/slice | solution.py:660
  117.5 2.3 %copy.13 = f32[32,32,256]{2,1,0:T(8,128)} copy(f32[32,32,256]{2,1,0:T(8,128)} %get-tuple-element.12) | data formatting | bytes 2097152
  119.8 2.3 %copy.14 = f32[32,32,256]{2,1,0:T(8,128)} copy(f32[32,32,256]{2,1,0:T(8,128)} %get-tuple-element.13) | data formatting | bytes 2097152

commit v4 on v3

--- a/solution.py
+++ b/solution.py
@@ -22,6 +22,7 @@
 PEOPLE = STACK * LOCAL
 PITCH = SIDE + 8
 TOGETHER = 8
+PIECES = 4
 LANES = 128
 CHUNKS = (4, 4, 4, 4, 4, 2, 2)
 SIDEWAYS = 8
@@ -427,7 +428,9 @@
         arrive(small_second_copies())
         total = small_mid[pl.ds(z * CLS_LOC, CLS_LOC), :] + small_second[0] + small_second[1] + small_second[2]
         norms = jnp.sum(total[:, :LANES], axis=1, keepdims=True)
-        norms_out[...] = jnp.broadcast_to(norms, (CLS_LOC, LANES))
+        lined = lax.broadcasted_iota(jnp.int32, (CLS_LOC, LANES), 0)
+        lined = lined == lax.broadcasted_iota(jnp.int32, (CLS_LOC, LANES), 1)
+        norms_out[...] = jnp.sum(jnp.where(lined, norms, 0.0), axis=0, keepdims=True)
         coef = total[:, LANES:LANES + GROUPS] + total[:, LANES + GROUPS:LANES + 2 * GROUPS]
 
         def weigh(r, carry):
@@ -599,6 +602,24 @@
             result_copy(which, block).wait()
 
 
+def hand_over(sums, weights, norms, sums_out, weights_out, norms_out, held, in_sem, out_sem):
+    size = CLS_LOC // PIECES
+    arriving, leaving = [], []
+    for n in range(PIECES):
+        part = pl.ds(n * size, size)
+        for which, (src, dst) in enumerate(((sums, sums_out), (weights, weights_out))):
+            arriving.append(pltpu.make_async_copy(src.at[part], held.at[which, part], in_sem.at[which, n]))
+            leaving.append(pltpu.make_async_copy(held.at[which, part], dst.at[part], out_sem.at[which, n]))
+    for copy in arriving:
+        copy.start()
+    norms_out[...] = norms[0, :CLS_LOC]
+    for here, there in zip(arriving, leaving):
+        here.wait()
+        there.start()
+    for copy in leaving:
+        copy.wait()
+
+
 def per_device(particles, classes, angles, groups, posterior, left_maps, right_maps, ctf_table):
     smem = pl.BlockSpec(memory_space=pltpu.SMEM)
     vmem = pl.BlockSpec(memory_space=pltpu.VMEM)
@@ -610,7 +631,7 @@
         out_shape=(
             jax.ShapeDtypeStruct((CLS_LOC, ROWS, SIDE), F32),
             jax.ShapeDtypeStruct((CLS_LOC, ROWS, SIDE), F32),
-            jax.ShapeDtypeStruct((CLS_LOC, LANES), F32),
+            jax.ShapeDtypeStruct((1, LANES), F32),
         ),
         in_specs=[smem, smem, vmem, vmem, vmem, hbm, hbm, hbm, hbm],
         out_specs=(hbm, hbm, vmem),
@@ -657,7 +678,16 @@
         ),
         name="class_sums",
     )(angles, groups, classes.reshape(1, LOCAL), groups.reshape(1, LOCAL), posterior.T, particles, left_maps, right_maps, ctf_table)
-    return (sums, weights, norms[:, 0])
+    shape = jax.ShapeDtypeStruct((CLS_LOC, ROWS, SIDE), F32)
+    return pl.pallas_call(
+        hand_over,
+        out_shape=(shape, shape, jax.ShapeDtypeStruct((CLS_LOC,), F32)),
+        in_specs=[hbm, hbm, vmem],
+        out_specs=(hbm, hbm, vmem),
+        scratch_shapes=[pltpu.VMEM((2, CLS_LOC, ROWS, SIDE), F32), dma((2, PIECES)), dma((2, PIECES))],
+        compiler_params=pltpu.CompilerParams(vmem_limit_bytes=8 * 1024 * 1024),
+        name="hand_over",
+    )(sums, weights, norms)
 
 
 def solution(mesh):

time: 122 us -> 122 us (level)
  Pallas kernels: 115 us -> 118 us
  local copies, waits for them, and re-layouts: 5.96 us -> 3.1 us
    pallas_call x0 -> x1, Pallas kernels: none -> 2.1 us  [per_device(): pl.pallas_call(hand_over, out_shape=(shape, shape, jax.ShapeDtypeStruct((...]
    unnamed x2 -> x6, local copies, waits for them, and re-layouts: 4.61 us -> 3.1 us
    slice x1 -> x0, local copies, waits for them, and re-layouts: 1.34 us -> none  [per_device(): return (sums, weights, norms[:, 0])]
where the time goes in v4:
time: 122 us; the launch traced here: 121 us
  Pallas kernels  118 us (97%)
  local copies, waits for them, and re-layouts  3.1 us (3%)
    pallas_call x1, Pallas kernels, per_device(): pl.pallas_call(body, out_shape=(jax.ShapeDtypeStruct((CLS_LOC, ROWS, SIDE...  115 us
    unnamed x6, local copies, waits for them, and re-layouts  3.1 us

profile of v4, /device:TPU:1, one launch (start us, length us, event | category | flops | bytes accessed | tf_op | source)
XLA Modules:
  0.0 121.5 jit_solution(10102981348481021467)
XLA Ops:
  0.6 115.5 %class_sums.1 = (f32[32,32,256]{2,1,0:T(8,128)}, f32[32,32,256]{2,1,0:T(8,128)}, f32[1,128]{1,0:T(1,128)}) custom-call(s32[64]{0:T(128)} %angles.1, s32[64]{0:T(128)} %groups.1, s32[1,64]{1,0:T(1,128)} %bitcast.4, s32[1,64]{1,0:T(1,128)} %bitcast.3, bf16[2,64]{1,0:T(2,128)(2,1)} %bitcast.5, bf16[64,256,256]{2,1,0:T(8,128)(2,1)} %particles.1, ...), custom_call_target="tpu_custom_call" | custom-call | tf_op jit(solution)/shard_map/class_sums/pallas_call | solution.py:629
  116.1 0.0 copy-start
  116.1 1.2 %copy-done = f32[32,32,256]{2,1,0:T(8,128)S(1)} copy-done((f32[32,32,256]{2,1,0:T(8,128)S(1)}, f32[32,32,256]{2,1,0:T(8,128)}, u32[]{:S(2)}) %copy-start) | copy-done | bytes 1048600
  117.4 0.0 copy-start.1
  117.4 1.2 %copy-done.1 = f32[32,32,256]{2,1,0:T(8,128)S(1)} copy-done((f32[32,32,256]{2,1,0:T(8,128)S(1)}, f32[32,32,256]{2,1,0:T(8,128)}, u32[]{:S(2)}) %copy-start.1) | copy-done | bytes 1048600
  118.6 0.0 copy-start.2
  118.6 0.7 copy-done.2
  119.2 2.1 %hand_over.1 = (f32[32,32,256]{2,1,0:T(8,128)}, f32[32,32,256]{2,1,0:T(8,128)}, f32[32]{0:T(128)}) custom-call(f32[32,32,256]{2,1,0:T(8,128)S(1)} %copy-done, f32[32,32,256]{2,1,0:T(8,128)S(1)} %copy-done.1, f32[1,128]{1,0:T(1,128)S(1)} %copy-done.2), custom_call_target="tpu_custom_call" | custom-call | tf_op jit(solution)/shard_map/hand_over/pallas_call | solution.py:682
Async XLA Ops:
  116.1 1.2 %copy-start = (f32[32,32,256]{2,1,0:T(8,128)S(1)}, f32[32,32,256]{2,1,0:T(8,128)}, u32[]{:S(2)}) copy-start(f32[32,32,256]{2,1,0:T(8,128)} %get-tuple-element.6.sums) | copy-start | bytes 3145732
  117.4 1.2 %copy-start.1 = (f32[32,32,256]{2,1,0:T(8,128)S(1)}, f32[32,32,256]{2,1,0:T(8,128)}, u32[]{:S(2)}) copy-start(f32[32,32,256]{2,1,0:T(8,128)} %get-tuple-element.7.weights) | copy-start | bytes 3145732
  118.6 0.7 copy-start.2

commit v5 on v4

--- a/solution.py
+++ b/solution.py
@@ -685,7 +685,7 @@
         in_specs=[hbm, hbm, vmem],
         out_specs=(hbm, hbm, vmem),
         scratch_shapes=[pltpu.VMEM((2, CLS_LOC, ROWS, SIDE), F32), dma((2, PIECES)), dma((2, PIECES))],
-        compiler_params=pltpu.CompilerParams(vmem_limit_bytes=8 * 1024 * 1024),
+        compiler_params=pltpu.CompilerParams(vmem_limit_bytes=63 * 1024 * 1024),
         name="hand_over",
     )(sums, weights, norms)
 

time: 122 us -> 120 us (0.984)
  local copies, waits for them, and re-layouts: 3.1 us -> 0 us
    unnamed x6 -> x0, local copies, waits for them, and re-layouts: 3.1 us -> none
    pallas_call x1, Pallas kernels: 2.1 us -> 3.54 us  [per_device(): pl.pallas_call(hand_over, out_shape=(shape, shape, jax.ShapeDtypeStruct((...]
where the time goes in v5:
time: 120 us
  Pallas kernels  119 us (99%)
    pallas_call x1, Pallas kernels, per_device(): pl.pallas_call(body, out_shape=(jax.ShapeDtypeStruct((CLS_LOC, ROWS, SIDE...  115 us
    pallas_call x1, Pallas kernels, per_device(): pl.pallas_call(hand_over, out_shape=(shape, shape, jax.ShapeDtypeStruct((...  3.54 us

profile of v5, /device:TPU:1, one launch (start us, length us, event | category | flops | bytes accessed | tf_op | source)
XLA Modules:
  0.0 119.6 jit_solution(8044595200070200444)
XLA Ops:
  0.6 115.5 %class_sums.1 = (f32[32,32,256]{2,1,0:T(8,128)}, f32[32,32,256]{2,1,0:T(8,128)}, f32[1,128]{1,0:T(1,128)}) custom-call(s32[64]{0:T(128)} %angles.1, s32[64]{0:T(128)} %groups.1, s32[1,64]{1,0:T(1,128)} %bitcast.4, s32[1,64]{1,0:T(1,128)} %bitcast.3, bf16[2,64]{1,0:T(2,128)(2,1)} %bitcast.5, bf16[64,256,256]{2,1,0:T(8,128)(2,1)} %particles.1, ...), custom_call_target="tpu_custom_call" | custom-call | tf_op jit(solution)/shard_map/class_sums/pallas_call | solution.py:629
  116.1 3.5 %hand_over.1 = (f32[32,32,256]{2,1,0:T(8,128)}, f32[32,32,256]{2,1,0:T(8,128)}, f32[32]{0:T(128)}) custom-call(f32[32,32,256]{2,1,0:T(8,128)} %get-tuple-element.6.sums, f32[32,32,256]{2,1,0:T(8,128)} %get-tuple-element.7.weights, f32[1,128]{1,0:T(1,128)} %get-tuple-element.8.norms), custom_call_target="tpu_custom_call" | custom-call | tf_op jit(solution)/shard_map/hand_over/pallas_call | solution.py:682

commit v6 on v5

--- a/solution.py
+++ b/solution.py
@@ -24,7 +24,7 @@
 TOGETHER = 8
 PIECES = 4
 LANES = 128
-CHUNKS = (4, 4, 4, 4, 4, 2, 2)
+CHUNKS = (4, 4, 4, 4, 4, 4)
 SIDEWAYS = 8
 SIDES = 2
 STRAIGHT = ROWS - SIDEWAYS

time: 120 us -> 123 us (1.025)
  Pallas kernels: 119 us -> 121 us
    pallas_call x1, Pallas kernels: 115 us -> 118 us  [per_device(): pl.pallas_call(body, out_shape=(jax.ShapeDtypeStruct((CLS_LOC, ROWS, SIDE...]
where the time goes in v6:
time: 123 us; the launch traced here: 122 us
  Pallas kernels  121 us (98%)
    pallas_call x1, Pallas kernels, per_device(): pl.pallas_call(body, out_shape=(jax.ShapeDtypeStruct((CLS_LOC, ROWS, SIDE...  118 us
    pallas_call x1, Pallas kernels, per_device(): pl.pallas_call(hand_over, out_shape=(shape, shape, jax.ShapeDtypeStruct((...  3.54 us

profile of v6, /device:TPU:1, one launch (start us, length us, event | category | flops | bytes accessed | tf_op | source)
XLA Modules:
  0.0 122.0 jit_solution(9194335098058232236)
XLA Ops:
  0.6 117.8 %class_sums.1 = (f32[32,32,256]{2,1,0:T(8,128)}, f32[32,32,256]{2,1,0:T(8,128)}, f32[1,128]{1,0:T(1,128)}) custom-call(s32[64]{0:T(128)} %angles.1, s32[64]{0:T(128)} %groups.1, s32[1,64]{1,0:T(1,128)} %bitcast.4, s32[1,64]{1,0:T(1,128)} %bitcast.3, bf16[2,64]{1,0:T(2,128)(2,1)} %bitcast.5, bf16[64,256,256]{2,1,0:T(8,128)(2,1)} %particles.1, ...), custom_call_target="tpu_custom_call" | custom-call | tf_op jit(solution)/shard_map/class_sums/pallas_call | solution.py:629
  118.5 3.5 %hand_over.1 = (f32[32,32,256]{2,1,0:T(8,128)}, f32[32,32,256]{2,1,0:T(8,128)}, f32[32]{0:T(128)}) custom-call(f32[32,32,256]{2,1,0:T(8,128)} %get-tuple-element.6.sums, f32[32,32,256]{2,1,0:T(8,128)} %get-tuple-element.7.weights, f32[1,128]{1,0:T(1,128)} %get-tuple-element.8.norms), custom_call_target="tpu_custom_call" | custom-call | tf_op jit(solution)/shard_map/hand_over/pallas_call | solution.py:682
